TPU v7x, 256 devices: a whole 4x4x8 slice. The times are simulated.
256 devices in a mesh: grp: 8 (over z), seq: 32 (over x, y, core).
Axes of the slice: x: 4, y: 4, z: 8, core: 2. Of those that a mesh axis runs over, the one named last changes fastest.
Arguments:
- queries: bfloat16 [8, 1024, 4096], P('grp', 'seq'), may hold values from -96 to 96
- attn_keys: bfloat16 [8, 1024, 4096], P('grp', 'seq'), may hold values from -4 to 4
- attn_values: bfloat16 [8, 1024, 4096], P('grp', 'seq'), may hold values from -6 to 6
- byte_grads: bfloat16 [8, 8192, 4096], P('grp', 'seq'), may hold values from -6 to 6
- seg_starts: int32 [8, 32, 32], P('grp', 'seq'), may hold values from 0 to 256, as said below
- up_gain: float32 [4096], replicated, may hold values from 0.1 to 1.9
Outputs:
- grad_queries: bfloat16 [8, 1024, 4096], P('grp', 'seq')
- grad_keys: bfloat16 [8, 1024, 4096], P('grp', 'seq')
- grad_values: bfloat16 [8, 1024, 4096], P('grp', 'seq')
- grad_gain: float32 [4096], P('seq')
Inputs may be any that keep to these rules, and one draw needn't show every extreme that they name: `seg_starts`: in every row each shard's entries rise strictly, the used ones below 256 and the unused slots after them equal to 256; every shard starts at least 8 segments and some shard of every row exactly 32; shard 0's first entry is 0.
All inputs are finite; a program needn't handle non-finite values.
Results may differ from a plain program's by a relative error of at most 0.012.
Values may be sent and summed in bfloat16 or wider, within the bound.
No kernel may reach another device: no remote copies, remote signals or barrier semaphores. Data moves between devices by JAX's collectives and lax.ppermute only.
A program may use at most 64 MiB of HBM per device.

v0:
```python
import math

import jax
import jax.numpy as jnp
from jax import lax
from jax.sharding import PartitionSpec as P

HD = 128


def shifted(value, axis, by):
    devices = lax.axis_size(axis)
    pairs = [(i, i + by) for i in range(devices) if 0 <= i + by < devices]
    return lax.ppermute(value, axis, pairs)


def shortened(value):
    return jax.tree.map(lambda a: a.astype(jnp.bfloat16) if a.dtype == jnp.float32 else a, value)


def head_grads(query_head, key_head, value_head, upstream, key_valid):
    seq_rows = query_head.shape[0]
    head_width = query_head.shape[1]
    block_rows = math.gcd(seq_rows, 512)
    block_total = seq_rows // block_rows
    scaling = 1.0 / math.sqrt(head_width)
    key_total = jnp.zeros((seq_rows, head_width), jnp.float32)
    value_total = jnp.zeros((seq_rows, head_width), jnp.float32)
    query_parts = []
    output_parts = []
    for block_index in range(block_total):
        first_row = block_index * block_rows
        prefix = first_row + block_rows
        query_block = query_head[first_row:prefix]
        upstream_block = upstream[first_row:prefix]
        key_prefix = key_head[:prefix]
        value_prefix = value_head[:prefix]
        scores = (
            jnp.einsum("qd,kd->qk", query_block, key_prefix, preferred_element_type=jnp.float32)
            * scaling
        )
        row_ids = first_row + jnp.arange(block_rows, dtype=jnp.int32)[:, None]
        col_ids = jnp.arange(prefix, dtype=jnp.int32)[None, :]
        allowed = (col_ids <= row_ids) & key_valid[None, :prefix]
        scores = jnp.where(allowed, scores, -1e30)
        row_max = jnp.max(scores, axis=1, keepdims=True)
        weights = jnp.exp(scores - row_max)
        attn_probs = weights / jnp.sum(weights, axis=1, keepdims=True)
        probs_low = attn_probs.astype(jnp.bfloat16)
        attn_out = jnp.einsum(
            "qk,kd->qd", probs_low, value_prefix, preferred_element_type=jnp.float32
        ).astype(jnp.bfloat16)
        grad_probs = jnp.einsum(
            "qd,kd->qk", upstream_block, value_prefix, preferred_element_type=jnp.float32
        )
        row_delta = jnp.sum(
            upstream_block.astype(jnp.float32) * attn_out.astype(jnp.float32), axis=1, keepdims=True
        )
        grad_scores = (attn_probs * (grad_probs - row_delta)).astype(jnp.bfloat16)
        grad_query = (
            jnp.einsum("qk,kd->qd", grad_scores, key_prefix, preferred_element_type=jnp.float32)
            * scaling
        ).astype(jnp.bfloat16)
        key_total = key_total.at[:prefix].add(
            jnp.einsum("qk,qd->kd", grad_scores, query_block, preferred_element_type=jnp.float32)
        )
        value_total = value_total.at[:prefix].add(
            jnp.einsum("qk,qd->kd", probs_low, upstream_block, preferred_element_type=jnp.float32)
        )
        query_parts.append(grad_query)
        output_parts.append(attn_out)
    grad_query = jnp.concatenate(query_parts, axis=0)
    attn_out = jnp.concatenate(output_parts, axis=0)
    grad_key = (key_total * scaling).astype(jnp.bfloat16)
    grad_value = value_total.astype(jnp.bfloat16)
    return (grad_query, grad_key, grad_value, attn_out)


def pool_bytes(byte_grads, seg_starts, slot_count):
    byte_count = byte_grads.shape[1]
    local_starts = seg_starts[0, 0]
    filled = jnp.sum((local_starts < byte_count).astype(jnp.int32))
    position = jnp.arange(byte_count, dtype=jnp.int32)
    started = jnp.sum((local_starts[None, :] <= position[:, None]).astype(jnp.int32), axis=1)
    slot_ids = jnp.arange(slot_count, dtype=jnp.int32)
    member = (started[None, :] - 1 == slot_ids[:, None]).astype(jnp.bfloat16)
    byte_rows = byte_grads[0]
    own_sums = jnp.dot(member, byte_rows, preferred_element_type=jnp.float32)
    leading = (started == 0).astype(jnp.bfloat16)[None, :]
    carried = jnp.dot(leading, byte_rows, preferred_element_type=jnp.float32)
    incoming = shifted(carried, "seq", -1)
    is_last = (slot_ids == filled - 1)[:, None]
    pooled = own_sums + jnp.where(is_last, incoming, 0.0)
    return pooled.astype(jnp.bfloat16)


def per_device(queries, attn_keys, attn_values, byte_grads, seg_starts, up_gain):
    slot_count = queries.shape[1]
    model_width = queries.shape[2]
    byte_count = byte_grads.shape[1]
    seq_count = lax.axis_size("seq")
    shard_index = lax.axis_index("seq")
    heads_here = model_width // (seq_count * HD)
    col_count = heads_here * HD
    all_starts = lax.all_gather(seg_starts[0], "seq", axis=0, tiled=True)
    key_valid = (all_starts < byte_count).reshape(-1)

    def by_heads(tensor):
        return tensor.reshape(slot_count, seq_count * heads_here, HD)

    pooled_low = pool_bytes(byte_grads, seg_starts, slot_count)
    head_query, head_key, head_value, head_pool = (
        lax.all_to_all(by_heads(queries[0]), "seq", split_axis=1, concat_axis=0, tiled=True),
        lax.all_to_all(by_heads(attn_keys[0]), "seq", split_axis=1, concat_axis=0, tiled=True),
        lax.all_to_all(by_heads(attn_values[0]), "seq", split_axis=1, concat_axis=0, tiled=True),
        lax.all_to_all(by_heads(pooled_low), "seq", split_axis=1, concat_axis=0, tiled=True),
    )
    gain_here = lax.dynamic_slice_in_dim(up_gain, shard_index * col_count, col_count).reshape(
        1, heads_here, HD
    )
    upstream = (gain_here * head_pool.astype(jnp.float32)).astype(jnp.bfloat16)

    def per_head(head_items):
        return head_grads(head_items[0], head_items[1], head_items[2], head_items[3], key_valid)

    stacked = tuple(
        (jnp.moveaxis(operand, 1, 0) for operand in (head_query, head_key, head_value, upstream))
    )
    results = lax.map(per_head, stacked)
    grad_query, grad_key, grad_value, attn_out = tuple(
        (jnp.moveaxis(operand, 0, 1) for operand in results)
    )

    def to_seq(tensor):
        return tensor.reshape(1, slot_count, model_width)

    returned = (
        lax.all_to_all(
            shortened(grad_query), "seq", split_axis=0, concat_axis=1, tiled=True
        ).astype(grad_query.dtype),
        lax.all_to_all(grad_key, "seq", split_axis=0, concat_axis=1, tiled=True),
        lax.all_to_all(grad_value, "seq", split_axis=0, concat_axis=1, tiled=True),
        lax.all_to_all(shortened(attn_out), "seq", split_axis=0, concat_axis=1, tiled=True).astype(
            attn_out.dtype
        ),
    )
    seq_out = returned[3].reshape(slot_count, model_width)
    seq_terms = jnp.sum(seq_out.astype(jnp.float32) * pooled_low.astype(jnp.float32), axis=0)
    gain_total = lax.psum(seq_terms, ("grp", "seq"))
    grad_gain = lax.dynamic_slice_in_dim(gain_total, shard_index * col_count, col_count)
    return (to_seq(returned[0]), to_seq(returned[1]), to_seq(returned[2]), grad_gain)


def solution(mesh):
    return jax.shard_map(
        per_device,
        mesh=mesh,
        in_specs=(
            P("grp", "seq", None),
            P("grp", "seq", None),
            P("grp", "seq", None),
            P("grp", "seq", None),
            P("grp", "seq", None),
            P(),
        ),
        out_specs=(P("grp", "seq", None), P("grp", "seq", None), P("grp", "seq", None), P("seq")),
        check_vma=False,
    )
```

profile of v0, /device:TPU:2, one launch (start us, length us, event | category | flops | bytes accessed | tf_op | source)
XLA Modules:
  0.0 224.5 jit_solution(2610333382745810122)
XLA Ops:
  0.7 1.1 copy.88
  1.8 0.8 copy.70
  2.6 7.6 %all-to-all-start = ((bf16[32,32,128]{2,0,1:T(8,128)(2,1)}), bf16[32,32,128]{2,0,1:T(8,128)(2,1)S(1)}, u32[]{:S(2)}, u32[]{:S(2)}) async-start(bf16[32,32,128]{2,0,1:T(8,128)(2,1)} %copy.70), calls=%async_computation | async-start | bytes 524288 | tf_op jit(solution)/shard_map/all_to_all | solution.py:113
  10.3 0.7 convert_reduce_fusion
  11.0 0.4 fusion
  11.4 4.3 %collective-permute-start = (f32[1,4096]{1,0:T(1,128)S(1)}, f32[1,4096]{1,0:T(1,128)S(1)}, u32[]{:S(2)}, u32[]{:S(2)}) collective-permute-start(f32[1,4096]{1,0:T(1,128)S(1)} %fusion), channel_id=1, source_target_pairs={{1,0},{2,1},{3,2},{4,3},{5,4},{6,5},{7,6},{8,7},{9,8},{10,9},{11,1... | collective-permute-start | bytes 49160 | tf_op jit(solution)/shard_map/ppermute | solution.py:14
  15.8 20.5 %all-gather = s32[32,1,32]{2,1,0:T(1,128)S(1)} all-gather(s32[1,1,32]{2,1,0:T(1,128)S(1)} %copy-done.19), channel_id=2, replica_groups=mesh['grp'=8,'seq'=32] {'seq'}, dimensions={0}, use_global_device_ids=true | all-gather | bytes 4224 | tf_op jit(solution)/shard_map/all_gather | solution.py:105
  36.3 0.6 fusion.29
  37.7 0.8 copy.71
  38.8 0.8 copy.73
  39.6 0.8 dynamic_slice.15
  40.3 0.5 add_convert_fusion
  40.8 6.8 %all-to-all-start.1 = ((bf16[32,32,128]{2,0,1:T(8,128)(2,1)}), bf16[32,32,128]{2,0,1:T(8,128)(2,1)S(1)}, u32[]{:S(2)}, u32[]{:S(2)}) async-start(bf16[32,32,128]{2,0,1:T(8,128)(2,1)} %copy.71), calls=%async_computation.1 | async-start | bytes 524288 | tf_op jit(solution)/shard_map/all_to_all | solution.py:114
  47.6 0.7 copy_bitcast_fusion
  48.4 6.9 %all-to-all-done.1 = bf16[32,32,128]{2,0,1:T(8,128)(2,1)S(1)} async-done(((bf16[32,32,128]{2,0,1:T(8,128)(2,1)}), bf16[32,32,128]{2,0,1:T(8,128)(2,1)S(1)}, u32[]{:S(2)}, u32[]{:S(2)}) %all-to-all-start.1) | async-done | bytes 262176 | tf_op jit(solution)/shard_map/all_to_all | solution.py:114
  55.3 5.0 %all-to-all-start.3 = ((bf16[32,32,128]{2,0,1:T(8,128)(2,1)}), bf16[32,32,128]{2,0,1:T(8,128)(2,1)S(1)}, u32[]{:S(2)}, u32[]{:S(2)}) async-start(bf16[32,32,128]{2,0,1:T(8,128)(2,1)} %copy.73), calls=%async_computation.3 | async-start | bytes 524288 | tf_op jit(solution)/shard_map/all_to_all | solution.py:115
  60.3 0.6 slice.137
  61.0 0.8 fusion.32
  61.7 0.5 fusion.6
  62.3 1.8 fusion.5
  64.0 4.1 %all-to-all-done.3 = bf16[32,32,128]{2,0,1:T(8,128)(2,1)S(1)} async-done(((bf16[32,32,128]{2,0,1:T(8,128)(2,1)}), bf16[32,32,128]{2,0,1:T(8,128)(2,1)S(1)}, u32[]{:S(2)}, u32[]{:S(2)}) %all-to-all-start.3) | async-done | bytes 262176 | tf_op jit(solution)/shard_map/all_to_all | solution.py:115
  68.1 5.7 %all-to-all-start.2 = ((bf16[32,32,128]{2,0,1:T(8,128)(2,1)}), bf16[32,32,128]{2,0,1:T(8,128)(2,1)}, u32[]{:S(2)}, u32[]{:S(2)}) async-start(bf16[32,32,128]{2,0,1:T(8,128)(2,1)} %copy_bitcast_fusion), calls=%async_computation.2 | async-start | bytes 524288 | tf_op jit(solution)/shard_map/all_to_all | solution.py:116
  73.8 0.7 slice.139
  74.5 1.3 fusion.33
  75.9 1.1 convolution_convert_fusion.1
  77.0 1.0 fusion.24
  78.0 3.7 %all-to-all-done.2 = bf16[32,32,128]{2,0,1:T(8,128)(2,1)} async-done(((bf16[32,32,128]{2,0,1:T(8,128)(2,1)}), bf16[32,32,128]{2,0,1:T(8,128)(2,1)}, u32[]{:S(2)}, u32[]{:S(2)}) %all-to-all-start.2) | async-done | bytes 262176 | tf_op jit(solution)/shard_map/all_to_all | solution.py:116
  81.6 1.0 bitcast_convert_fusion
  82.7 2.2 multiply_reduce_fusion.1
  85.0 0.3 fusion.9
  85.6 0.5 copy-done.6
  86.1 0.6 copy-done.2
  86.8 0.4 multiply_convert_fusion
  87.2 1.1 fusion.16
  88.3 0.5 fusion.13
  88.8 0.5 broadcast.160
  89.3 0.8 reduce.17
  90.2 0.8 reshape.259
  90.9 5.0 %all-to-all-start.5 = ((bf16[32,2,2048]{2,1,0:T(2,128)(2,1)}), bf16[32,2,2048]{2,1,0:T(2,128)(2,1)S(1)}, u32[]{:S(2)}, u32[]{:S(2)}) async-start(bf16[32,2,2048]{2,1,0:T(2,128)(2,1)} %reshape.259), calls=%async_computation.5 | async-start | bytes 524288 | tf_op jit(solution)/shard_map/all_to_all | solution.py:141
  96.0 0.3 fusion.15
  96.4 1.0 maximum_bitcast_fusion
  97.4 1.5 reduce.16
  98.8 1.7 reshape.257
  100.6 3.2 %all-to-all-done.5 = bf16[32,2,2048]{2,1,0:T(2,128)(2,1)S(1)} async-done(((bf16[32,2,2048]{2,1,0:T(2,128)(2,1)}), bf16[32,2,2048]{2,1,0:T(2,128)(2,1)S(1)}, u32[]{:S(2)}, u32[]{:S(2)}) %all-to-all-start.5) | async-done | bytes 262176 | tf_op jit(solution)/shard_map/all_to_all | solution.py:141
  103.8 5.0 %all-to-all-start.4 = ((bf16[32,2,2048]{2,1,0:T(2,128)(2,1)}), bf16[32,2,2048]{2,1,0:T(2,128)(2,1)S(1)}, u32[]{:S(2)}, u32[]{:S(2)}) async-start(bf16[32,2,2048]{2,1,0:T(2,128)(2,1)} %reshape.257), calls=%async_computation.4 | async-start | bytes 524288 | tf_op jit(solution)/shard_map/all_to_all | solution.py:138
  108.8 1.6 maximum_bitcast_fusion.1
  110.4 2.4 %reduce.19 = bf16[1024,128]{1,0:T(8,128)(2,1)} reduce(bf16[1024,1,128]{2,0,1:T(8,128)(2,1)} %maximum_bitcast_fusion.1, bf16[]{:T(256)} %broadcast.160), dimensions={1}, to_apply=%copy.81.reduce_sub_computation | reduce | bytes 524290 | tf_op jit(solution)/shard_map/transpose | solution.py:131
  112.8 1.7 reshape.263
  114.6 2.0 all-to-all-done.4
  116.6 5.7 %all-to-all-start.7 = ((bf16[32,2,2048]{2,1,0:T(2,128)(2,1)}), bf16[32,2,2048]{2,1,0:T(2,128)(2,1)}, u32[]{:S(2)}, u32[]{:S(2)}) async-start(bf16[32,2,2048]{2,1,0:T(2,128)(2,1)} %reshape.263), calls=%async_computation.7 | async-start | bytes 524288 | tf_op jit(solution)/shard_map/all_to_all | solution.py:143
  122.6 2.1 fusion.14
  124.7 0.8 reduce.18
  125.5 0.8 reshape.261
  126.3 3.9 %all-to-all-done.7 = bf16[32,2,2048]{2,1,0:T(2,128)(2,1)} async-done(((bf16[32,2,2048]{2,1,0:T(2,128)(2,1)}), bf16[32,2,2048]{2,1,0:T(2,128)(2,1)}, u32[]{:S(2)}, u32[]{:S(2)}) %all-to-all-start.7) | async-done | bytes 262176 | tf_op jit(solution)/shard_map/all_to_all | solution.py:143
  130.1 5.9 %all-to-all-start.6 = ((bf16[32,2,2048]{2,1,0:T(2,128)(2,1)}), bf16[32,2,2048]{2,1,0:T(2,128)(2,1)}, u32[]{:S(2)}, u32[]{:S(2)}) async-start(bf16[32,2,2048]{2,1,0:T(2,128)(2,1)} %reshape.261), calls=%async_computation.6 | async-start | bytes 524288 | tf_op jit(solution)/shard_map/all_to_all | solution.py:142
  136.4 0.8 reshape.241
  137.7 0.8 reshape.240
  138.5 2.2 reshape.264
  140.7 0.5 convert_element_type.145
  141.5 0.3 fusion.20
  141.9 78.9 %psum.7 = f32[4096]{0:T(1024)S(1)} all-reduce(f32[4096]{0:T(1024)S(1)} %fusion.20), channel_id=1, replica_groups=mesh['grp'=8,'seq'=32] {'grp','seq'}, use_global_device_ids=true, to_apply=%region_9.10 | all-reduce | flops 4096 | bytes 32768 | tf_op jit(solution)/shard_map/psum | solution.py:149
  220.7 0.6 dynamic_slice.16
  221.3 2.2 reshape.262
  223.6 0.8 reshape.242
  (66 shorter events, 2.6 us)
Async XLA Ops:
  0.6 10.4 %copy-start = (bf16[1,256,4096]{2,1,0:T(8,128)(2,1)S(1)}, bf16[1,256,4096]{2,1,0:T(8,128)(2,1)}, u32[]{:S(2)}) copy-start(bf16[1,256,4096]{2,1,0:T(8,128)(2,1)} %param.21) | copy-start | bytes 6291460
  0.6 15.1 %copy-start.19 = (s32[1,1,32]{2,1,0:T(1,128)S(1)}, s32[1,1,32]{2,1,0:T(1,128)}, u32[]{:S(2)}) copy-start(s32[1,1,32]{2,1,0:T(1,128)} %param.22) | copy-start | bytes 388
  0.7 37.0 %copy-start.16 = (bf16[1,32,4096]{2,1,0:T(8,128)(2,1)S(1)}, bf16[1,32,4096]{2,1,0:T(8,128)(2,1)}, u32[]{:S(2)}) copy-start(bf16[1,32,4096]{2,1,0:T(8,128)(2,1)} %param.19) | copy-start | bytes 786436
  1.8 36.9 %copy-start.17 = (bf16[1,32,4096]{2,1,0:T(8,128)(2,1)S(1)}, bf16[1,32,4096]{2,1,0:T(8,128)(2,1)}, u32[]{:S(2)}) copy-start(bf16[1,32,4096]{2,1,0:T(8,128)(2,1)} %param.20) | copy-start | bytes 786436
  2.6 38.2 %all-to-all-start = ((bf16[32,32,128]{2,0,1:T(8,128)(2,1)}), bf16[32,32,128]{2,0,1:T(8,128)(2,1)S(1)}, u32[]{:S(2)}, u32[]{:S(2)}) async-start(bf16[32,32,128]{2,0,1:T(8,128)(2,1)} %copy.70), calls=%async_computation | async-start | bytes 524288 | tf_op jit(solution)/shard_map/all_to_all | solution.py:113
  11.4 28.9 %collective-permute-start = (f32[1,4096]{1,0:T(1,128)S(1)}, f32[1,4096]{1,0:T(1,128)S(1)}, u32[]{:S(2)}, u32[]{:S(2)}) collective-permute-start(f32[1,4096]{1,0:T(1,128)S(1)} %fusion), channel_id=1, source_target_pairs={{1,0},{2,1},{3,2},{4,3},{5,4},{6,5},{7,6},{8,7},{9,8},{10,9},{11,1... | collective-permute-start | bytes 49160 | tf_op jit(solution)/shard_map/ppermute | solution.py:14
  40.8 21.0 %copy-start.3 = (bf16[32,4096]{1,0:T(8,128)(2,1)}, bf16[32,4096]{1,0:T(8,128)(2,1)S(1)}, u32[]{:S(2)}) copy-start(bf16[32,4096]{1,0:T(8,128)(2,1)S(1)} %add_convert_fusion) | copy-start | bytes 786436
  40.8 14.5 %all-to-all-start.1 = ((bf16[32,32,128]{2,0,1:T(8,128)(2,1)}), bf16[32,32,128]{2,0,1:T(8,128)(2,1)S(1)}, u32[]{:S(2)}, u32[]{:S(2)}) async-start(bf16[32,32,128]{2,0,1:T(8,128)(2,1)} %copy.71), calls=%async_computation.1 | async-start | bytes 524288 | tf_op jit(solution)/shard_map/all_to_all | solution.py:114
  48.4 13.9 %copy-start.14 = (bf16[16,32,1,128]{3,1,0,2:T(8,128)(2,1)}, bf16[16,32,1,128]{3,1,0,2:T(8,128)(2,1)S(1)}, u32[]{:S(2)}) copy-start(bf16[16,32,1,128]{3,1,0,2:T(8,128)(2,1)S(1)} %get-tuple-element.124) | copy-start | bytes 393220
  55.3 7.0 %copy-start.8 = (bf16[32,32,128]{2,0,1:T(8,128)(2,1)}, bf16[32,32,128]{2,0,1:T(8,128)(2,1)S(1)}, u32[]{:S(2)}) copy-start(bf16[32,32,128]{2,0,1:T(8,128)(2,1)S(1)} %all-to-all-done.1) | copy-start | bytes 786436
  55.3 12.8 %all-to-all-start.3 = ((bf16[32,32,128]{2,0,1:T(8,128)(2,1)}), bf16[32,32,128]{2,0,1:T(8,128)(2,1)S(1)}, u32[]{:S(2)}, u32[]{:S(2)}) async-start(bf16[32,32,128]{2,0,1:T(8,128)(2,1)} %copy.73), calls=%async_computation.3 | async-start | bytes 524288 | tf_op jit(solution)/shard_map/all_to_all | solution.py:115
  68.1 13.5 %all-to-all-start.2 = ((bf16[32,32,128]{2,0,1:T(8,128)(2,1)}), bf16[32,32,128]{2,0,1:T(8,128)(2,1)}, u32[]{:S(2)}, u32[]{:S(2)}) async-start(bf16[32,32,128]{2,0,1:T(8,128)(2,1)} %copy_bitcast_fusion), calls=%async_computation.2 | async-start | bytes 524288 | tf_op jit(solution)/shard_map/all_to_all | solution.py:116
  73.8 2.1 copy-start.1
  81.6 3.3 %copy-start.18 = (bf16[16,32,1,128]{3,1,0,2:T(8,128)(2,1)S(1)}, bf16[16,32,1,128]{3,1,0,2:T(8,128)(2,1)}, u32[]{:S(2)}) copy-start(bf16[16,32,1,128]{3,1,0,2:T(8,128)(2,1)} %slice.139) | copy-start | bytes 393220
  82.7 3.4 %copy-start.10 = (bf16[1024,1,128]{2,0,1:T(8,128)(2,1)}, bf16[1024,1,128]{2,0,1:T(8,128)(2,1)S(1)}, u32[]{:S(2)}) copy-start(bf16[1024,1,128]{2,0,1:T(8,128)(2,1)S(1)} %fusion.21) | copy-start | bytes 786436
  85.0 1.8 copy-start.2
  85.3 0.8 copy-start.6
  85.3 1.9 copy-start.9
  86.8 1.6 copy-start.15
  87.2 8.8 %copy-start.7 = (bf16[512,512]{0,1:T(8,128)(2,1)S(1)}, bf16[512,512]{0,1:T(8,128)(2,1)}, u32[]{:S(2)}) copy-start(bf16[512,512]{0,1:T(8,128)(2,1)} %copy-done.6) | copy-start | bytes 1572868
  87.2 8.8 %copy-start.13 = (bf16[16,32,1,128]{3,1,0,2:T(8,128)(2,1)S(1)}, bf16[16,32,1,128]{3,1,0,2:T(8,128)(2,1)}, u32[]{:S(2)}) copy-start(bf16[16,32,1,128]{3,1,0,2:T(8,128)(2,1)} %slice.137) | copy-start | bytes 393220
  90.2 18.6 %copy-start.12 = (bf16[512,128]{1,0:T(8,128)(2,1)S(1)}, bf16[512,128]{1,0:T(8,128)(2,1)}, u32[]{:S(2)}) copy-start(bf16[512,128]{1,0:T(8,128)(2,1)} %convolution_convert_fusion.1) | copy-start | bytes 393220
  90.9 12.8 %all-to-all-start.5 = ((bf16[32,2,2048]{2,1,0:T(2,128)(2,1)}), bf16[32,2,2048]{2,1,0:T(2,128)(2,1)S(1)}, u32[]{:S(2)}, u32[]{:S(2)}) async-start(bf16[32,2,2048]{2,1,0:T(2,128)(2,1)} %reshape.259), calls=%async_computation.5 | async-start | bytes 524288 | tf_op jit(solution)/shard_map/all_to_all | solution.py:141
  96.3 25.9 %copy-start.5 = (bf16[512,512]{0,1:T(8,128)(2,1)S(1)}, bf16[512,512]{0,1:T(8,128)(2,1)}, u32[]{:S(2)}) copy-start(bf16[512,512]{0,1:T(8,128)(2,1)} %fusion.24) | copy-start | bytes 1572868
  96.4 25.9 %copy-start.11 = (bf16[1024,1,128]{2,0,1:T(8,128)(2,1)S(1)}, bf16[1024,1,128]{2,0,1:T(8,128)(2,1)}, u32[]{:S(2)}) copy-start(bf16[1024,1,128]{2,0,1:T(8,128)(2,1)} %copy-done.10) | copy-start | bytes 786436
  103.8 12.8 %all-to-all-start.4 = ((bf16[32,2,2048]{2,1,0:T(2,128)(2,1)}), bf16[32,2,2048]{2,1,0:T(2,128)(2,1)S(1)}, u32[]{:S(2)}, u32[]{:S(2)}) async-start(bf16[32,2,2048]{2,1,0:T(2,128)(2,1)} %reshape.257), calls=%async_computation.4 | async-start | bytes 524288 | tf_op jit(solution)/shard_map/all_to_all | solution.py:138
  116.6 13.5 %all-to-all-start.7 = ((bf16[32,2,2048]{2,1,0:T(2,128)(2,1)}), bf16[32,2,2048]{2,1,0:T(2,128)(2,1)}, u32[]{:S(2)}, u32[]{:S(2)}) async-start(bf16[32,2,2048]{2,1,0:T(2,128)(2,1)} %reshape.263), calls=%async_computation.7 | async-start | bytes 524288 | tf_op jit(solution)/shard_map/all_to_all | solution.py:143
  130.1 91.2 %all-to-all-start.6 = ((bf16[32,2,2048]{2,1,0:T(2,128)(2,1)}), bf16[32,2,2048]{2,1,0:T(2,128)(2,1)}, u32[]{:S(2)}, u32[]{:S(2)}) async-start(bf16[32,2,2048]{2,1,0:T(2,128)(2,1)} %reshape.261), calls=%async_computation.6 | async-start | bytes 524288 | tf_op jit(solution)/shard_map/all_to_all | solution.py:142
  137.6 4.0 %copy-start.4 = (bf16[32,4096]{1,0:T(8,128)(2,1)S(1)}, bf16[32,4096]{1,0:T(8,128)(2,1)}, u32[]{:S(2)}) copy-start(bf16[32,4096]{1,0:T(8,128)(2,1)} %copy-done.3) | copy-start | bytes 786436
where the time goes:
time: 229 us; the launch traced here: 224 us
  blocking collectives  99.3 us (43%)
  starting transfers between devices  51 us (22%)
  waiting for transfers between devices  23.8 us (10%)
  local copies, waits for them, and re-layouts  22 us (10%)
  other arithmetic  15 us (7%)
  matrix products  11.5 us (5%)
    psum x1, blocking collectives, per_device(): gain_total = lax.psum(seq_terms, ('grp', 'seq'))  78.9 us
    all_gather x1, blocking collectives, per_device(): all_starts = lax.all_gather(seg_starts[0], 'seq', axis=0, tiled=True)  20.5 us
    unnamed x54, local copies, waits for them, and re-layouts  12.4 us
    transpose x6, other arithmetic, per_device(): jnp.moveaxis(operand, 0, 1)  8.13 us
    all_to_all x1, starting transfers between devices, per_device(): lax.all_to_all(by_heads(queries[0]), 'seq', split_axis=1, concat_axis=0,...  7.62 us
    all_to_all x1, waiting for transfers between devices, per_device(): lax.all_to_all(by_heads(attn_keys[0]), 'seq', split_axis=1, concat_axis=0...  6.94 us
    all_to_all x1, starting transfers between devices, per_device(): lax.all_to_all(by_heads(attn_keys[0]), 'seq', split_axis=1, concat_axis=0...  6.77 us
    all_to_all x1, starting transfers between devices, per_device(): lax.all_to_all(grad_value, 'seq', split_axis=0, concat_axis=1, tiled=True)  5.85 us
  transfers between devices with their start and end apart: 9, of which 6 were waited for; matrix products, arithmetic and copies ran while one was open for 15% of the time, Pallas kernels for 0%

commit v1 on v0

v1 whole, which is shorter than its diff:
```python
import functools
import math

import jax
import jax.numpy as jnp
from jax import lax
from jax.experimental import pallas as pl
from jax.experimental.pallas import tpu as pltpu
from jax.sharding import PartitionSpec as P

HD = 128
EXTRA = 16


def start_columns(starts, byte_count):
    count = starts.shape[1]
    row = lax.broadcasted_iota(jnp.int32, (count, count), 0)
    col = lax.broadcasted_iota(jnp.int32, (count, count), 1)
    spread = jnp.broadcast_to(starts, (count, count))
    begin = jnp.sum(jnp.where(row == col, spread, 0), axis=1, keepdims=True)
    end = jnp.sum(jnp.where(row + 1 == col, spread, 0), axis=1, keepdims=True)
    last_row = lax.broadcasted_iota(jnp.int32, (count, 1), 0) == count - 1
    return begin, jnp.where(last_row, byte_count, end)


def pack_kernel(query_ref, key_ref, value_ref, bytes_ref, starts_ref, packed_ref):
    heads = packed_ref.shape[0]
    slots = query_ref.shape[1]
    byte_count = bytes_ref.shape[1]
    starts = starts_ref[0].astype(jnp.float32)
    begin, end = start_columns(starts, float(byte_count))
    position = lax.broadcasted_iota(jnp.int32, (slots, byte_count), 1).astype(jnp.float32)
    own = (begin <= position) & (position < end)
    filled = jnp.sum(jnp.where(starts < byte_count, 1.0, 0.0), axis=1, keepdims=True)
    first = jnp.min(starts, axis=1, keepdims=True)
    last = jnp.max(jnp.where(starts < byte_count, starts, -1.0), axis=1, keepdims=True)
    row = lax.broadcasted_iota(jnp.int32, (EXTRA, byte_count), 0)
    place = lax.broadcasted_iota(jnp.int32, (EXTRA, byte_count), 1).astype(jnp.float32)
    leading = (row < 2) & (place < first)
    tail = (row == 2) & (place >= last)
    member = jnp.concatenate(
        [jnp.where(own, 1.0, 0.0), jnp.where(leading | tail, 1.0, 0.0)], axis=0
    ).astype(jnp.bfloat16)
    sums = jnp.dot(member, bytes_ref[0], preferred_element_type=jnp.float32)
    extra = sums[slots:]
    low = extra - extra.astype(jnp.bfloat16).astype(jnp.float32)
    kind = lax.broadcasted_iota(jnp.int32, extra.shape, 0)
    extra = jnp.where(kind == 0, extra, jnp.where(kind == 3, filled, low)).astype(jnp.bfloat16)
    pooled = sums[:slots].astype(jnp.bfloat16)
    for head in range(heads):
        cols = slice(head * HD, (head + 1) * HD)
        packed_ref[head, 0:slots, :] = query_ref[0, :, cols]
        packed_ref[head, slots : 2 * slots, :] = key_ref[0, :, cols]
        packed_ref[head, 2 * slots : 3 * slots, :] = value_ref[0, :, cols]
        packed_ref[head, 3 * slots : 4 * slots, :] = pooled[:, cols]
        packed_ref[head, 4 * slots :, :] = extra[:, cols]


def pack(queries, attn_keys, attn_values, byte_grads, seg_starts, steps):
    slots, width = queries.shape[1:]
    byte_count = byte_grads.shape[1]
    cap = seg_starts.shape[2]
    cols = width // steps
    heads = width // HD
    rows = 4 * slots + EXTRA
    slot_spec = pl.BlockSpec((1, slots, cols), lambda i: (0, 0, i))
    return pl.pallas_call(
        pack_kernel,
        grid=(steps,),
        in_specs=[
            slot_spec,
            slot_spec,
            slot_spec,
            pl.BlockSpec((1, byte_count, cols), lambda i: (0, 0, i)),
            pl.BlockSpec((1, 1, cap), lambda i: (0, 0, 0)),
        ],
        out_specs=pl.BlockSpec((heads // steps, rows, HD), lambda i: (i, 0, 0)),
        out_shape=jax.ShapeDtypeStruct((heads, rows, HD), jnp.bfloat16),
        compiler_params=pltpu.CompilerParams(vmem_limit_bytes=32 * 2**20),
        name="pool_and_pack",
    )(queries, attn_keys, attn_values, byte_grads, seg_starts)


def attention_kernel(
    block, packed_ref, gain_ref, grads_ref, gain_grad_ref, upstream_ref, pooled_ref, bias_ref, dk_ref, dv_ref
):
    shards, rows, width = packed_ref.shape
    slots = (rows - EXTRA) // 4
    total = shards * slots
    scaling = 1.0 / math.sqrt(width)

    extra = packed_ref[:, 4 * slots :, :].astype(jnp.float32)
    carried = extra[:, 0:1, :] + extra[:, 1:2, :]
    incoming = jnp.concatenate([carried[1:], jnp.zeros_like(carried[:1])], axis=0)
    incoming = incoming + extra[:, 2:3, :]
    filled = extra[:, 3:4, :]
    slot = lax.broadcasted_iota(jnp.int32, (shards, slots, width), 1).astype(jnp.float32)
    pooled = packed_ref[:, 3 * slots : 4 * slots, :].astype(jnp.float32)
    pooled = pooled + jnp.where(slot == filled - 1.0, incoming, 0.0)
    pooled = pooled.reshape(total, width).astype(jnp.bfloat16)
    pooled_ref[...] = pooled
    upstream_ref[...] = (gain_ref[...] * pooled.astype(jnp.float32)).astype(jnp.bfloat16)
    bias_ref[...] = jnp.where(slot < filled, 0.0, -1e30).reshape(total, width)

    query = packed_ref[:, 0:slots, :].reshape(total, width)
    key = packed_ref[:, slots : 2 * slots, :].reshape(total, width)
    value = packed_ref[:, 2 * slots : 3 * slots, :].reshape(total, width)
    key_t = key.T
    value_t = value.T
    gain_grad = jnp.zeros((1, width), jnp.float32)
    contract_last = (((1,), (1,)), ((), ()))
    for index in range(total // block):
        first = index * block
        prefix = first + block
        query_block = query[first:prefix]
        upstream_block = upstream_ref[first:prefix]
        scores = lax.dot_general(
            key[:prefix], query_block, contract_last, preferred_element_type=jnp.float32
        )
        bias = jnp.concatenate([bias_ref[:prefix]] * (block // width), axis=1)
        scores = scores + bias
        key_ids = lax.broadcasted_iota(jnp.int32, (block, block), 0)
        query_ids = lax.broadcasted_iota(jnp.int32, (block, block), 1)
        diagonal = jnp.where(key_ids <= query_ids, scores[first:], -1e30)
        scores = jnp.concatenate([scores[:first], diagonal], axis=0) if first else diagonal
        row_max = jnp.max(scores, axis=0, keepdims=True)
        weights = jnp.exp((scores - row_max) * scaling)
        probs = weights * (1.0 / jnp.sum(weights, axis=0, keepdims=True))
        probs_low = probs.astype(jnp.bfloat16)
        out_t = jnp.dot(value_t[:, :prefix], probs_low, preferred_element_type=jnp.float32)
        out_t = out_t.astype(jnp.bfloat16).astype(jnp.float32)
        upstream_t = upstream_block.astype(jnp.float32).T
        row_delta = jnp.sum(upstream_t * out_t, axis=0, keepdims=True)
        gain_grad += jnp.sum(
            out_t.T * pooled_ref[first:prefix].astype(jnp.float32), axis=0, keepdims=True
        )
        grad_probs = lax.dot_general(
            value[:prefix], upstream_block, contract_last, preferred_element_type=jnp.float32
        )
        grad_scores = (probs * (grad_probs - row_delta)).astype(jnp.bfloat16)
        dq_t = jnp.dot(key_t[:, :prefix], grad_scores, preferred_element_type=jnp.float32)
        dq = (dq_t.T * scaling).astype(jnp.bfloat16)
        owners = slice(first // slots, prefix // slots)
        grads_ref[owners, 0:slots, :] = dq.reshape(block // slots, slots, width)
        dk = jnp.dot(grad_scores, query_block, preferred_element_type=jnp.float32)
        dv = jnp.dot(probs_low, upstream_block, preferred_element_type=jnp.float32)
        if first:
            dk_ref[:first] += dk[:first]
            dv_ref[:first] += dv[:first]
        dk_ref[first:prefix] = dk[first:]
        dv_ref[first:prefix] = dv[first:]
    grads_ref[:, slots : 2 * slots, :] = (
        (dk_ref[...] * scaling).astype(jnp.bfloat16).reshape(shards, slots, width)
    )
    grads_ref[:, 2 * slots :, :] = dv_ref[...].astype(jnp.bfloat16).reshape(shards, slots, width)
    gain_grad_ref[...] = gain_grad


def attention(packed, gain, block):
    shards, rows, width = packed.shape
    slots = (rows - EXTRA) // 4
    total = shards * slots
    vmem = pl.BlockSpec(memory_space=pltpu.VMEM)
    return pl.pallas_call(
        functools.partial(attention_kernel, block),
        in_specs=[vmem, vmem],
        out_specs=[vmem, vmem],
        out_shape=[
            jax.ShapeDtypeStruct((shards, 3 * slots, width), jnp.bfloat16),
            jax.ShapeDtypeStruct((1, width), jnp.float32),
        ],
        scratch_shapes=[
            pltpu.VMEM((total, width), jnp.bfloat16),
            pltpu.VMEM((total, width), jnp.bfloat16),
            pltpu.VMEM((total, width), jnp.float32),
            pltpu.VMEM((total, width), jnp.float32),
            pltpu.VMEM((total, width), jnp.float32),
        ],
        compiler_params=pltpu.CompilerParams(vmem_limit_bytes=40 * 2**20),
        name="attention_grads",
    )(packed, gain)


def unpack_kernel(grads_ref, dq_ref, dk_ref, dv_ref):
    slots = dq_ref.shape[1]
    for head in range(grads_ref.shape[0]):
        cols = slice(head * HD, (head + 1) * HD)
        dq_ref[0, :, cols] = grads_ref[head, 0:slots, :]
        dk_ref[0, :, cols] = grads_ref[head, slots : 2 * slots, :]
        dv_ref[0, :, cols] = grads_ref[head, 2 * slots :, :]


def unpack(grads):
    heads, rows, width = grads.shape
    out = jax.ShapeDtypeStruct((1, rows // 3, heads * width), jnp.bfloat16)
    vmem = pl.BlockSpec(memory_space=pltpu.VMEM)
    return pl.pallas_call(
        unpack_kernel,
        in_specs=[vmem],
        out_specs=[vmem] * 3,
        out_shape=[out] * 3,
        compiler_params=pltpu.CompilerParams(vmem_limit_bytes=16 * 2**20),
        name="unpack_grads",
    )(grads)


def group_sum(value):
    count = lax.axis_size("grp")
    step = 1
    while step < count:
        value = value + lax.ppermute(value, "grp", [(i, i ^ step) for i in range(count)])
        step *= 2
    return value


def per_device(queries, attn_keys, attn_values, byte_grads, seg_starts, up_gain):
    packed = pack(queries, attn_keys, attn_values, byte_grads, seg_starts, 4)
    received = lax.all_to_all(packed, "seq", split_axis=0, concat_axis=0, tiled=True)
    gain = lax.dynamic_slice_in_dim(up_gain.reshape(-1, HD), lax.axis_index("seq"), 1)
    grads, gain_grad = attention(received, gain, 256)
    returned = lax.all_to_all(grads, "seq", split_axis=0, concat_axis=0, tiled=True)
    dq, dk, dv = unpack(returned)
    return dq, dk, dv, group_sum(gain_grad).reshape(HD)


def solution(mesh):
    rows = P("grp", "seq", None)
    return jax.shard_map(
        per_device,
        mesh=mesh,
        in_specs=(rows, rows, rows, rows, rows, P()),
        out_specs=(rows, rows, rows, P("seq")),
        check_vma=False,
    )
```

time: 229 us -> 62.1 us (0.27); the launches traced: 224 us -> 61.7 us
  blocking collectives: 99.3 us -> 0 us
  starting transfers between devices: 51 us -> 26.2 us
  local copies, waits for them, and re-layouts: 22 us -> 5.11 us
  other arithmetic: 15 us -> 0.52 us
  matrix products: 11.5 us -> 0 us
  Pallas kernels: 0 us -> 8.75 us
  waiting for transfers between devices: 23.8 us -> 20.5 us
    psum x1 -> x0, blocking collectives: 78.9 us -> none  [per_device(): gain_total = lax.psum(seq_terms, ('grp', 'seq'))]
    all_to_all x8 -> x2, starting transfers between devices: 46.6 us -> 14.1 us  [the longest x1 7.62 us: per_device(): lax.all_to_all(packed, 'seq', split_axis=0, concat_axis=0, tiled=True)]
    all_gather x1 -> x0, blocking collectives: 20.5 us -> none  [per_device(): all_starts = lax.all_gather(seg_starts[0], 'seq', axis=0, tiled=True)]
    dot_general x14 -> x0, matrix products: 11.5 us -> none  [the longest x2 3.33 us: head_grads(): jnp.einsum('qk,kd->qd', probs_low, value_prefix, preferred_element_type=j...]
    pallas_call x0 -> x3, Pallas kernels: none -> 8.75 us  [the longest x1 5.35 us: attention(): pl.pallas_call(functools.partial(attention_kernel, block), in_specs=[vmem...]
    transpose x6 -> x0, other arithmetic: 8.13 us -> none  [per_device(): jnp.moveaxis(operand, 0, 1)]
    all_to_all x8 -> x2, waiting for transfers between devices: 23.8 us -> 15.8 us  [the longest x1 15.8 us: per_device(): lax.all_to_all(packed, 'seq', split_axis=0, concat_axis=0, tiled=True)]
    ppermute x1 -> x3, starting transfers between devices: 4.33 us -> 12.1 us  [group_sum(): lax.ppermute(value, 'grp', [(i, i ^ step) for i in range(count)])]
  transfers between devices with their start and end apart: 9 -> 5, of which waited for: 6 -> 4; matrix products, arithmetic and copies ran while one was open for 15% -> 1% of each run, Pallas kernels for 0% -> 0%
where the time goes in v1:
time: 62.1 us; the launch traced here: 61.7 us
  starting transfers between devices  26.2 us (42%)
  waiting for transfers between devices  20.5 us (33%)
  Pallas kernels  8.75 us (14%)
  local copies, waits for them, and re-layouts  5.11 us (8%)
  between operations  0.69 us (1%)
    all_to_all x1, waiting for transfers between devices, per_device(): lax.all_to_all(packed, 'seq', split_axis=0, concat_axis=0, tiled=True)  15.8 us
    ppermute x3, starting transfers between devices, group_sum(): lax.ppermute(value, 'grp', [(i, i ^ step) for i in range(count)])  12.1 us
    all_to_all x1, starting transfers between devices, per_device(): lax.all_to_all(packed, 'seq', split_axis=0, concat_axis=0, tiled=True)  7.62 us
    all_to_all x1, starting transfers between devices, per_device(): lax.all_to_all(grads, 'seq', split_axis=0, concat_axis=0, tiled=True)  6.43 us
    pallas_call x1, Pallas kernels, attention(): pl.pallas_call(functools.partial(attention_kernel, block), in_specs=[vmem...  5.35 us
    unnamed x12, local copies, waits for them, and re-layouts  5.1 us
    ppermute x3, waiting for transfers between devices, group_sum(): lax.ppermute(value, 'grp', [(i, i ^ step) for i in range(count)])  4.66 us
    pallas_call x1, Pallas kernels, pack(): pl.pallas_call(pack_kernel, grid=(steps,), in_specs=[slot_spec, slot_spec...  2.38 us
  transfers between devices with their start and end apart: 5, of which 4 were waited for; matrix products, arithmetic and copies ran while one was open for 1% of the time, Pallas kernels for 0%

profile of v1, /device:TPU:2, one launch (start us, length us, event | category | flops | bytes accessed | tf_op | source)
XLA Modules:
  0.0 61.7 jit_solution(16215639142842710491)
XLA Ops:
  0.6 0.0 copy-start
  0.6 0.0 copy-start.1
  0.7 1.6 %copy-done.1 = bf16[1,256,4096]{2,1,0:T(8,128)(2,1)S(1)} copy-done((bf16[1,256,4096]{2,1,0:T(8,128)(2,1)S(1)}, bf16[1,256,4096]{2,1,0:T(8,128)(2,1)}, u32[]{:S(2)}) %copy-start.1) | copy-done | bytes 2097176
  2.2 0.0 copy-start.2
  2.2 0.9 %copy-done.2 = bf16[1,32,4096]{2,1,0:T(8,128)(2,1)S(1)} copy-done((bf16[1,32,4096]{2,1,0:T(8,128)(2,1)S(1)}, bf16[1,32,4096]{2,1,0:T(8,128)(2,1)}, u32[]{:S(2)}) %copy-start.2) | copy-done | bytes 262168
  3.2 0.0 copy-start.3
  3.2 0.9 %copy-done.3 = bf16[1,32,4096]{2,1,0:T(8,128)(2,1)S(1)} copy-done((bf16[1,32,4096]{2,1,0:T(8,128)(2,1)S(1)}, bf16[1,32,4096]{2,1,0:T(8,128)(2,1)}, u32[]{:S(2)}) %copy-start.3) | copy-done | bytes 262168
  4.1 0.0 copy-start.4
  4.1 0.9 %copy-done.4 = bf16[1,32,4096]{2,1,0:T(8,128)(2,1)S(1)} copy-done((bf16[1,32,4096]{2,1,0:T(8,128)(2,1)S(1)}, bf16[1,32,4096]{2,1,0:T(8,128)(2,1)}, u32[]{:S(2)}) %copy-start.4) | copy-done | bytes 262168
  5.1 0.0 copy-start.5
  5.1 0.7 %copy-done.5 = s32[1,1,32]{2,1,0:T(1,128)S(1)} copy-done((s32[1,1,32]{2,1,0:T(1,128)S(1)}, s32[1,1,32]{2,1,0:T(1,128)}, u32[]{:S(2)}) %copy-start.5) | copy-done | bytes 152
  5.8 2.4 %pool_and_pack.1 = bf16[32,144,128]{2,1,0:T(8,128)(2,1)} custom-call(bf16[1,32,4096]{2,1,0:T(8,128)(2,1)S(1)} %copy-done.2, bf16[1,32,4096]{2,1,0:T(8,128)(2,1)S(1)} %copy-done.3, bf16[1,32,4096]{2,1,0:T(8,128)(2,1)S(1)} %copy-done.4, bf16[1,256,4096]{2,1,0:T(8,128)(2,1)S(1)} %copy-done.1, s32[1,1,32]{2,1,0:T(1,128)S(1)} %copy-done.5), custom_call_target="tpu_custom_call" | custom-call | tf_op jit(solution)/shard_map/pool_and_pack/pallas_call | solution.py:67
  8.1 7.6 %all-to-all-start = ((bf16[32,144,128]{2,1,0:T(8,128)(2,1)}), bf16[32,144,128]{2,1,0:T(8,128)(2,1)S(1)}, u32[]{:S(2)}, u32[]{:S(2)}) async-start(bf16[32,144,128]{2,1,0:T(8,128)(2,1)} %pool_and_pack.1), calls=%async_computation | async-start | bytes 2359296 | tf_op jit(solution)/shard_map/all_to_all | solution.py:218
  15.8 0.0 copy-done
  15.8 15.8 %all-to-all-done.packed_ref = bf16[32,144,128]{2,1,0:T(8,128)(2,1)S(1)} async-done(((bf16[32,144,128]{2,1,0:T(8,128)(2,1)}), bf16[32,144,128]{2,1,0:T(8,128)(2,1)S(1)}, u32[]{:S(2)}, u32[]{:S(2)}) %all-to-all-start) | async-done | bytes 1179680 | tf_op jit(solution)/shard_map/all_to_all | solution.py:218
  31.6 5.3 %attention_grads.1 = (bf16[32,96,128]{2,1,0:T(8,128)(2,1)}, f32[1,128]{1,0:T(1,128)S(1)}) custom-call(bf16[32,144,128]{2,1,0:T(8,128)(2,1)S(1)} %all-to-all-done.packed_ref, f32[1,128]{1,0:T(1,128)S(1)} %constant_dynamic-slice_fusion.gain_ref), custom_call_target="tpu_custom_call" | custom-call | tf_op jit(solution)/shard_map/attention_grads/pallas_call | solution.py:164
  37.0 6.4 %all-to-all-start.1 = ((bf16[32,96,128]{2,1,0:T(8,128)(2,1)}), bf16[32,96,128]{2,1,0:T(8,128)(2,1)S(1)}, u32[]{:S(2)}, u32[]{:S(2)}) async-start(bf16[32,96,128]{2,1,0:T(8,128)(2,1)} %get-tuple-element.9), calls=%async_computation.1 | async-start | bytes 1572864 | tf_op jit(solution)/shard_map/all_to_all | solution.py:221
  43.4 2.0 %collective-permute-start = (f32[1,128]{1,0:T(1,128)S(1)}, f32[1,128]{1,0:T(1,128)S(1)}, u32[]{:S(2)}, u32[]{:S(2)}) collective-permute-start(f32[1,128]{1,0:T(1,128)S(1)} %get-tuple-element.13), channel_id=1, source_target_pairs={{0,32},{32,0},{64,96},{96,64},{128,160},{160,128},{192,224},{224,1... | collective-permute-start | bytes 1544 | tf_op jit(solution)/shard_map/ppermute | solution.py:211
  45.4 1.6 %collective-permute-done = f32[1,128]{1,0:T(1,128)S(1)} collective-permute-done((f32[1,128]{1,0:T(1,128)S(1)}, f32[1,128]{1,0:T(1,128)S(1)}, u32[]{:S(2)}, u32[]{:S(2)}) %collective-permute-start) | collective-permute-done | bytes 544 | tf_op jit(solution)/shard_map/ppermute | solution.py:211
  47.0 3.3 %collective-permute-start.1 = (f32[1,128]{1,0:T(1,128)S(1)}, f32[1,128]{1,0:T(1,128)S(1)}, u32[]{:S(2)}, u32[]{:S(2)}) collective-permute-start(f32[1,128]{1,0:T(1,128)S(1)} %add.13), channel_id=1, source_target_pairs={{0,64},{32,96},{64,0},{96,32},{128,192},{160,224},{192,128},{224,1... | collective-permute-start | bytes 1544 | tf_op jit(solution)/shard_map/ppermute | solution.py:211
  50.3 1.5 %collective-permute-done.1 = f32[1,128]{1,0:T(1,128)S(1)} collective-permute-done((f32[1,128]{1,0:T(1,128)S(1)}, f32[1,128]{1,0:T(1,128)S(1)}, u32[]{:S(2)}, u32[]{:S(2)}) %collective-permute-start.1) | collective-permute-done | bytes 544 | tf_op jit(solution)/shard_map/ppermute | solution.py:211
  51.8 6.8 %collective-permute-start.2 = (f32[1,128]{1,0:T(1,128)S(1)}, f32[1,128]{1,0:T(1,128)S(1)}, u32[]{:S(2)}, u32[]{:S(2)}) collective-permute-start(f32[1,128]{1,0:T(1,128)S(1)} %add.14), channel_id=1, source_target_pairs={{0,128},{32,160},{64,192},{96,224},{128,0},{160,32},{192,64},{224,... | collective-permute-start | bytes 1544 | tf_op jit(solution)/shard_map/ppermute | solution.py:211
  58.7 1.5 %collective-permute-done.2 = f32[1,128]{1,0:T(1,128)S(1)} collective-permute-done((f32[1,128]{1,0:T(1,128)S(1)}, f32[1,128]{1,0:T(1,128)S(1)}, u32[]{:S(2)}, u32[]{:S(2)}) %collective-permute-start.2) | collective-permute-done | bytes 544 | tf_op jit(solution)/shard_map/ppermute | solution.py:211
  60.2 0.5 add_bitcast_fusion
  60.7 0.0 all-to-all-done.1.grads_ref
  60.7 1.0 %unpack_grads.1 = (bf16[1,32,4096]{2,1,0:T(8,128)(2,1)}, bf16[1,32,4096]{2,1,0:T(8,128)(2,1)}, bf16[1,32,4096]{2,1,0:T(8,128)(2,1)}) custom-call(bf16[32,96,128]{2,1,0:T(8,128)(2,1)S(1)} %all-to-all-done.1.grads_ref), custom_call_target="tpu_custom_call" | custom-call | tf_op jit(solution)/shard_map/unpack_grads/pallas_call | solution.py:197
  (3 shorter events, 0.0 us)
Async XLA Ops:
  0.6 15.1 %copy-start = (f32[4096]{0:T(1024)S(1)}, f32[4096]{0:T(1024)}, u32[]{:S(2)}) copy-start(f32[4096]{0:T(1024)} %param.11) | copy-start | bytes 49156
  0.6 1.6 %copy-start.1 = (bf16[1,256,4096]{2,1,0:T(8,128)(2,1)S(1)}, bf16[1,256,4096]{2,1,0:T(8,128)(2,1)}, u32[]{:S(2)}) copy-start(bf16[1,256,4096]{2,1,0:T(8,128)(2,1)} %bytes_ref.1) | copy-start | bytes 6291460
  2.2 0.9 %copy-start.2 = (bf16[1,32,4096]{2,1,0:T(8,128)(2,1)S(1)}, bf16[1,32,4096]{2,1,0:T(8,128)(2,1)}, u32[]{:S(2)}) copy-start(bf16[1,32,4096]{2,1,0:T(8,128)(2,1)} %query_ref.1) | copy-start | bytes 786436
  3.2 0.9 %copy-start.3 = (bf16[1,32,4096]{2,1,0:T(8,128)(2,1)S(1)}, bf16[1,32,4096]{2,1,0:T(8,128)(2,1)}, u32[]{:S(2)}) copy-start(bf16[1,32,4096]{2,1,0:T(8,128)(2,1)} %key_ref.1) | copy-start | bytes 786436
  4.1 0.9 %copy-start.4 = (bf16[1,32,4096]{2,1,0:T(8,128)(2,1)S(1)}, bf16[1,32,4096]{2,1,0:T(8,128)(2,1)}, u32[]{:S(2)}) copy-start(bf16[1,32,4096]{2,1,0:T(8,128)(2,1)} %value_ref.1) | copy-start | bytes 786436
  5.1 0.7 %copy-start.5 = (s32[1,1,32]{2,1,0:T(1,128)S(1)}, s32[1,1,32]{2,1,0:T(1,128)}, u32[]{:S(2)}) copy-start(s32[1,1,32]{2,1,0:T(1,128)} %starts_ref.1) | copy-start | bytes 388
  8.1 23.5 %all-to-all-start = ((bf16[32,144,128]{2,1,0:T(8,128)(2,1)}), bf16[32,144,128]{2,1,0:T(8,128)(2,1)S(1)}, u32[]{:S(2)}, u32[]{:S(2)}) async-start(bf16[32,144,128]{2,1,0:T(8,128)(2,1)} %pool_and_pack.1), calls=%async_computation | async-start | bytes 2359296 | tf_op jit(solution)/shard_map/all_to_all | solution.py:218
  37.0 23.7 %all-to-all-start.1 = ((bf16[32,96,128]{2,1,0:T(8,128)(2,1)}), bf16[32,96,128]{2,1,0:T(8,128)(2,1)S(1)}, u32[]{:S(2)}, u32[]{:S(2)}) async-start(bf16[32,96,128]{2,1,0:T(8,128)(2,1)} %get-tuple-element.9), calls=%async_computation.1 | async-start | bytes 1572864 | tf_op jit(solution)/shard_map/all_to_all | solution.py:221
  43.4 3.6 %collective-permute-start = (f32[1,128]{1,0:T(1,128)S(1)}, f32[1,128]{1,0:T(1,128)S(1)}, u32[]{:S(2)}, u32[]{:S(2)}) collective-permute-start(f32[1,128]{1,0:T(1,128)S(1)} %get-tuple-element.13), channel_id=1, source_target_pairs={{0,32},{32,0},{64,96},{96,64},{128,160},{160,128},{192,224},{224,1... | collective-permute-start | bytes 1544 | tf_op jit(solution)/shard_map/ppermute | solution.py:211
  47.0 4.8 %collective-permute-start.1 = (f32[1,128]{1,0:T(1,128)S(1)}, f32[1,128]{1,0:T(1,128)S(1)}, u32[]{:S(2)}, u32[]{:S(2)}) collective-permute-start(f32[1,128]{1,0:T(1,128)S(1)} %add.13), channel_id=1, source_target_pairs={{0,64},{32,96},{64,0},{96,32},{128,192},{160,224},{192,128},{224,1... | collective-permute-start | bytes 1544 | tf_op jit(solution)/shard_map/ppermute | solution.py:211
  51.8 8.4 %collective-permute-start.2 = (f32[1,128]{1,0:T(1,128)S(1)}, f32[1,128]{1,0:T(1,128)S(1)}, u32[]{:S(2)}, u32[]{:S(2)}) collective-permute-start(f32[1,128]{1,0:T(1,128)S(1)} %add.14), channel_id=1, source_target_pairs={{0,128},{32,160},{64,192},{96,224},{128,0},{160,32},{192,64},{224,... | collective-permute-start | bytes 1544 | tf_op jit(solution)/shard_map/ppermute | solution.py:211

commit v2 on v1

--- a/solution.py
+++ b/solution.py
@@ -9,7 +9,7 @@
 from jax.sharding import PartitionSpec as P
 
 HD = 128
-EXTRA = 16
+EXTRA = 8
 
 
 def start_columns(starts, byte_count):
@@ -76,13 +76,24 @@
         ],
         out_specs=pl.BlockSpec((heads // steps, rows, HD), lambda i: (i, 0, 0)),
         out_shape=jax.ShapeDtypeStruct((heads, rows, HD), jnp.bfloat16),
-        compiler_params=pltpu.CompilerParams(vmem_limit_bytes=32 * 2**20),
+        compiler_params=pltpu.CompilerParams(vmem_limit_bytes=60 * 2**20),
         name="pool_and_pack",
     )(queries, attn_keys, attn_values, byte_grads, seg_starts)
 
 
 def attention_kernel(
-    block, packed_ref, gain_ref, grads_ref, gain_grad_ref, upstream_ref, pooled_ref, bias_ref, dk_ref, dv_ref
+    block,
+    packed_ref,
+    gain_ref,
+    grads_ref,
+    gain_grad_ref,
+    upstream_ref,
+    pooled_ref,
+    bias_ref,
+    dk_ref,
+    dv_ref,
+    staged_ref,
+    sems,
 ):
     shards, rows, width = packed_ref.shape
     slots = (rows - EXTRA) // 4
@@ -109,7 +120,9 @@
     value_t = value.T
     gain_grad = jnp.zeros((1, width), jnp.float32)
     contract_last = (((1,), (1,)), ((), ()))
-    for index in range(total // block):
+    blocks = total // block
+    copies = []
+    for index in reversed(range(blocks)):
         first = index * block
         prefix = first + block
         query_block = query[first:prefix]
@@ -139,21 +152,33 @@
         )
         grad_scores = (probs * (grad_probs - row_delta)).astype(jnp.bfloat16)
         dq_t = jnp.dot(key_t[:, :prefix], grad_scores, preferred_element_type=jnp.float32)
-        dq = (dq_t.T * scaling).astype(jnp.bfloat16)
-        owners = slice(first // slots, prefix // slots)
-        grads_ref[owners, 0:slots, :] = dq.reshape(block // slots, slots, width)
         dk = jnp.dot(grad_scores, query_block, preferred_element_type=jnp.float32)
         dv = jnp.dot(probs_low, upstream_block, preferred_element_type=jnp.float32)
-        if first:
+        dk_own, dv_own = dk[first:], dv[first:]
+        if index < blocks - 1:
+            dk_own = dk_own + dk_ref[first:prefix]
+            dv_own = dv_own + dv_ref[first:prefix]
+        if first and index < blocks - 1:
             dk_ref[:first] += dk[:first]
             dv_ref[:first] += dv[:first]
-        dk_ref[first:prefix] = dk[first:]
-        dv_ref[first:prefix] = dv[first:]
-    grads_ref[:, slots : 2 * slots, :] = (
-        (dk_ref[...] * scaling).astype(jnp.bfloat16).reshape(shards, slots, width)
-    )
-    grads_ref[:, 2 * slots :, :] = dv_ref[...].astype(jnp.bfloat16).reshape(shards, slots, width)
+        elif first:
+            dk_ref[:first] = dk[:first]
+            dv_ref[:first] = dv[:first]
+        owners = slice(first // slots, prefix // slots)
+        shape = (block // slots, slots, width)
+        staged_ref[owners, 0:slots, :] = (dq_t.T * scaling).astype(jnp.bfloat16).reshape(shape)
+        staged_ref[owners, slots : 2 * slots, :] = (
+            (dk_own * scaling).astype(jnp.bfloat16).reshape(shape)
+        )
+        staged_ref[owners, 2 * slots :, :] = dv_own.astype(jnp.bfloat16).reshape(shape)
+        copy = pltpu.make_async_copy(
+            staged_ref.at[owners], grads_ref.at[owners], sems.at[index]
+        )
+        copy.start()
+        copies.append(copy)
     gain_grad_ref[...] = gain_grad
+    for copy in copies:
+        copy.wait()
 
 
 def attention(packed, gain, block):
@@ -164,7 +189,7 @@
     return pl.pallas_call(
         functools.partial(attention_kernel, block),
         in_specs=[vmem, vmem],
-        out_specs=[vmem, vmem],
+        out_specs=[pl.BlockSpec(memory_space=pl.ANY), vmem],
         out_shape=[
             jax.ShapeDtypeStruct((shards, 3 * slots, width), jnp.bfloat16),
             jax.ShapeDtypeStruct((1, width), jnp.float32),
@@ -175,6 +200,8 @@
             pltpu.VMEM((total, width), jnp.float32),
             pltpu.VMEM((total, width), jnp.float32),
             pltpu.VMEM((total, width), jnp.float32),
+            pltpu.VMEM((shards, 3 * slots, width), jnp.bfloat16),
+            pltpu.SemaphoreType.DMA((total // block,)),
         ],
         compiler_params=pltpu.CompilerParams(vmem_limit_bytes=40 * 2**20),
         name="attention_grads",
@@ -204,23 +231,25 @@
     )(grads)
 
 
-def group_sum(value):
+def group_half(value, step):
     count = lax.axis_size("grp")
-    step = 1
-    while step < count:
-        value = value + lax.ppermute(value, "grp", [(i, i ^ step) for i in range(count)])
-        step *= 2
-    return value
+    return lax.ppermute(value, "grp", [(i, i ^ step) for i in range(count)])
 
 
 def per_device(queries, attn_keys, attn_values, byte_grads, seg_starts, up_gain):
-    packed = pack(queries, attn_keys, attn_values, byte_grads, seg_starts, 4)
+    packed = pack(queries, attn_keys, attn_values, byte_grads, seg_starts, 2)
     received = lax.all_to_all(packed, "seq", split_axis=0, concat_axis=0, tiled=True)
     gain = lax.dynamic_slice_in_dim(up_gain.reshape(-1, HD), lax.axis_index("seq"), 1)
-    grads, gain_grad = attention(received, gain, 256)
+    grads, gain_grad = attention(received, gain, 512)
     returned = lax.all_to_all(grads, "seq", split_axis=0, concat_axis=0, tiled=True)
+    step = lax.axis_size("grp") // 2
+    while step > 1:
+        gain_grad = gain_grad + group_half(gain_grad, step)
+        step //= 2
+    other = group_half(gain_grad, step)
     dq, dk, dv = unpack(returned)
-    return dq, dk, dv, group_sum(gain_grad).reshape(HD)
+    gain_grad, dv = lax.optimization_barrier((gain_grad, dv))
+    return dq, dk, dv, (gain_grad + other).reshape(HD)
 
 
 def solution(mesh):

time: 62.1 us -> 54.6 us (0.88)
  local copies, waits for them, and re-layouts: 5.11 us -> 0.02 us
  starting transfers between devices: 26.2 us -> 24.4 us
    unnamed x12 -> x2, local copies, waits for them, and re-layouts: 5.1 us -> 0.01 us
    ppermute x3, starting transfers between devices: 12.1 us -> 10.3 us  [group_half(): return lax.ppermute(value, 'grp', [(i, i ^ step) for i in range(count)])]
    pallas_call x1, Pallas kernels: 5.35 us -> 4.07 us  [attention(): pl.pallas_call(functools.partial(attention_kernel, block), in_specs=[vmem...]
    ppermute x3, waiting for transfers between devices: 4.66 us -> 5.45 us  [group_half(): return lax.ppermute(value, 'grp', [(i, i ^ step) for i in range(count)])]
    all_to_all x1, waiting for transfers between devices: 15.8 us -> 15.1 us  [per_device(): lax.all_to_all(packed, 'seq', split_axis=0, concat_axis=0, tiled=True)]
    pallas_call x1, Pallas kernels: 2.38 us -> 3.06 us  [pack(): pl.pallas_call(pack_kernel, grid=(steps,), in_specs=[slot_spec, slot_spec...]
  transfers between devices with their start and end apart: 5 -> 5, of which waited for: 4 -> 4; matrix products, arithmetic and copies ran while one was open for 1% -> 0% of each run, Pallas kernels for 0% -> 2%
where the time goes in v2:
time: 54.6 us; the launch traced here: 54.3 us
  starting transfers between devices  24.4 us (45%)
  waiting for transfers between devices  20.6 us (38%)
  Pallas kernels  8.14 us (15%)
  between operations  0.69 us (1%)
    all_to_all x1, waiting for transfers between devices, per_device(): lax.all_to_all(packed, 'seq', split_axis=0, concat_axis=0, tiled=True)  15.1 us
    ppermute x3, starting transfers between devices, group_half(): return lax.ppermute(value, 'grp', [(i, i ^ step) for i in range(count)])  10.3 us
    all_to_all x1, starting transfers between devices, per_device(): lax.all_to_all(packed, 'seq', split_axis=0, concat_axis=0, tiled=True)  7.62 us
    all_to_all x1, starting transfers between devices, per_device(): lax.all_to_all(grads, 'seq', split_axis=0, concat_axis=0, tiled=True)  6.44 us
    ppermute x3, waiting for transfers between devices, group_half(): return lax.ppermute(value, 'grp', [(i, i ^ step) for i in range(count)])  5.45 us
    pallas_call x1, Pallas kernels, attention(): pl.pallas_call(functools.partial(attention_kernel, block), in_specs=[vmem...  4.07 us
    pallas_call x1, Pallas kernels, pack(): pl.pallas_call(pack_kernel, grid=(steps,), in_specs=[slot_spec, slot_spec...  3.06 us
  transfers between devices with their start and end apart: 5, of which 4 were waited for; matrix products, arithmetic and copies ran while one was open for 0% of the time, Pallas kernels for 2%

profile of v2, /device:TPU:2, one launch (start us, length us, event | category | flops | bytes accessed | tf_op | source)
XLA Modules:
  0.0 54.3 jit_solution(14662635560964542380)
XLA Ops:
  0.6 0.0 copy-start
  0.6 3.1 %pool_and_pack.1 = bf16[32,136,128]{2,1,0:T(8,128)(2,1)} custom-call(bf16[1,32,4096]{2,1,0:T(8,128)(2,1)} %query_ref.1, bf16[1,32,4096]{2,1,0:T(8,128)(2,1)} %key_ref.1, bf16[1,32,4096]{2,1,0:T(8,128)(2,1)} %value_ref.1, bf16[1,256,4096]{2,1,0:T(8,128)(2,1)} %bytes_ref.1, s32[1,1,32]{2,1,0:T(1,128)} %starts_ref.1), custom_call_target="tpu_custom_call" | custom-call | tf_op jit(solution)/shard_map/pool_and_pack/pallas_call | solution.py:67
  3.7 7.6 %all-to-all-start = ((bf16[32,136,128]{2,1,0:T(8,128)(2,1)}), bf16[32,136,128]{2,1,0:T(8,128)(2,1)S(1)}, u32[]{:S(2)}, u32[]{:S(2)}) async-start(bf16[32,136,128]{2,1,0:T(8,128)(2,1)} %pool_and_pack.1), calls=%async_computation | async-start | bytes 2228224 | tf_op jit(solution)/shard_map/all_to_all | solution.py:241
  11.3 0.0 copy-done
  11.4 15.1 %all-to-all-done.packed_ref = bf16[32,136,128]{2,1,0:T(8,128)(2,1)S(1)} async-done(((bf16[32,136,128]{2,1,0:T(8,128)(2,1)}), bf16[32,136,128]{2,1,0:T(8,128)(2,1)S(1)}, u32[]{:S(2)}, u32[]{:S(2)}) %all-to-all-start) | async-done | bytes 1114144 | tf_op jit(solution)/shard_map/all_to_all | solution.py:241
  26.5 4.1 %attention_grads.1 = (bf16[32,96,128]{2,1,0:T(8,128)(2,1)}, f32[1,128]{1,0:T(1,128)S(1)}) custom-call(bf16[32,136,128]{2,1,0:T(8,128)(2,1)S(1)} %all-to-all-done.packed_ref, f32[1,128]{1,0:T(1,128)S(1)} %constant_dynamic-slice_fusion.gain_ref), custom_call_target="tpu_custom_call" | custom-call | tf_op jit(solution)/shard_map/attention_grads/pallas_call | solution.py:189
  30.5 6.4 %all-to-all-start.1 = ((bf16[32,96,128]{2,1,0:T(8,128)(2,1)}), bf16[32,96,128]{2,1,0:T(8,128)(2,1)S(1)}, u32[]{:S(2)}, u32[]{:S(2)}) async-start(bf16[32,96,128]{2,1,0:T(8,128)(2,1)} %get-tuple-element.11), calls=%async_computation.1 | async-start | bytes 1572864 | tf_op jit(solution)/shard_map/all_to_all | solution.py:244
  37.0 7.3 %collective-permute-start = (f32[1,128]{1,0:T(1,128)S(1)}, f32[1,128]{1,0:T(1,128)S(1)}, u32[]{:S(2)}, u32[]{:S(2)}) collective-permute-start(f32[1,128]{1,0:T(1,128)S(1)} %get-tuple-element.14), channel_id=1, source_target_pairs={{0,128},{32,160},{64,192},{96,224},{128,0},{160,32},{192,64},{224,... | collective-permute-start | bytes 1544 | tf_op jit(solution)/shard_map/ppermute | solution.py:236
  44.3 1.5 %collective-permute-done = f32[1,128]{1,0:T(1,128)S(1)} collective-permute-done((f32[1,128]{1,0:T(1,128)S(1)}, f32[1,128]{1,0:T(1,128)S(1)}, u32[]{:S(2)}, u32[]{:S(2)}) %collective-permute-start) | collective-permute-done | bytes 544 | tf_op jit(solution)/shard_map/ppermute | solution.py:236
  45.8 2.0 %collective-permute-start.1 = (f32[1,128]{1,0:T(1,128)S(1)}, f32[1,128]{1,0:T(1,128)S(1)}, u32[]{:S(2)}, u32[]{:S(2)}) collective-permute-start(f32[1,128]{1,0:T(1,128)S(1)} %add.13), channel_id=1, source_target_pairs={{0,64},{32,96},{64,0},{96,32},{128,192},{160,224},{192,128},{224,1... | collective-permute-start | bytes 1544 | tf_op jit(solution)/shard_map/ppermute | solution.py:236
  47.8 2.4 %collective-permute-done.1 = f32[1,128]{1,0:T(1,128)S(1)} collective-permute-done((f32[1,128]{1,0:T(1,128)S(1)}, f32[1,128]{1,0:T(1,128)S(1)}, u32[]{:S(2)}, u32[]{:S(2)}) %collective-permute-start.1) | collective-permute-done | bytes 544 | tf_op jit(solution)/shard_map/ppermute | solution.py:236
  50.2 1.0 %collective-permute-start.2 = (f32[1,128]{1,0:T(1,128)S(1)}, f32[1,128]{1,0:T(1,128)S(1)}, u32[]{:S(2)}, u32[]{:S(2)}) collective-permute-start(f32[1,128]{1,0:T(1,128)S(1)} %add.14), channel_id=1, source_target_pairs={{0,32},{32,0},{64,96},{96,64},{128,160},{160,128},{192,224},{224,1... | collective-permute-start | bytes 1544 | tf_op jit(solution)/shard_map/ppermute | solution.py:236
  51.3 0.0 all-to-all-done.1.grads_ref
  51.3 1.0 %unpack_grads.1 = (bf16[1,32,4096]{2,1,0:T(8,128)(2,1)}, bf16[1,32,4096]{2,1,0:T(8,128)(2,1)}, bf16[1,32,4096]{2,1,0:T(8,128)(2,1)}) custom-call(bf16[32,96,128]{2,1,0:T(8,128)(2,1)S(1)} %all-to-all-done.1.grads_ref), custom_call_target="tpu_custom_call" | custom-call | tf_op jit(solution)/shard_map/unpack_grads/pallas_call | solution.py:224
  52.3 1.5 %collective-permute-done.2 = f32[1,128]{1,0:T(1,128)S(1)} collective-permute-done((f32[1,128]{1,0:T(1,128)S(1)}, f32[1,128]{1,0:T(1,128)S(1)}, u32[]{:S(2)}, u32[]{:S(2)}) %collective-permute-start.2) | collective-permute-done | bytes 544 | tf_op jit(solution)/shard_map/ppermute | solution.py:236
  53.8 0.5 add_bitcast_fusion
  (3 shorter events, 0.0 us)
Async XLA Ops:
  0.6 10.7 %copy-start = (f32[4096]{0:T(1024)S(1)}, f32[4096]{0:T(1024)}, u32[]{:S(2)}) copy-start(f32[4096]{0:T(1024)} %param.11) | copy-start | bytes 49156
  3.7 22.8 %all-to-all-start = ((bf16[32,136,128]{2,1,0:T(8,128)(2,1)}), bf16[32,136,128]{2,1,0:T(8,128)(2,1)S(1)}, u32[]{:S(2)}, u32[]{:S(2)}) async-start(bf16[32,136,128]{2,1,0:T(8,128)(2,1)} %pool_and_pack.1), calls=%async_computation | async-start | bytes 2228224 | tf_op jit(solution)/shard_map/all_to_all | solution.py:241
  30.5 20.7 %all-to-all-start.1 = ((bf16[32,96,128]{2,1,0:T(8,128)(2,1)}), bf16[32,96,128]{2,1,0:T(8,128)(2,1)S(1)}, u32[]{:S(2)}, u32[]{:S(2)}) async-start(bf16[32,96,128]{2,1,0:T(8,128)(2,1)} %get-tuple-element.11), calls=%async_computation.1 | async-start | bytes 1572864 | tf_op jit(solution)/shard_map/all_to_all | solution.py:244
  37.0 8.8 %collective-permute-start = (f32[1,128]{1,0:T(1,128)S(1)}, f32[1,128]{1,0:T(1,128)S(1)}, u32[]{:S(2)}, u32[]{:S(2)}) collective-permute-start(f32[1,128]{1,0:T(1,128)S(1)} %get-tuple-element.14), channel_id=1, source_target_pairs={{0,128},{32,160},{64,192},{96,224},{128,0},{160,32},{192,64},{224,... | collective-permute-start | bytes 1544 | tf_op jit(solution)/shard_map/ppermute | solution.py:236
  45.8 4.4 %collective-permute-start.1 = (f32[1,128]{1,0:T(1,128)S(1)}, f32[1,128]{1,0:T(1,128)S(1)}, u32[]{:S(2)}, u32[]{:S(2)}) collective-permute-start(f32[1,128]{1,0:T(1,128)S(1)} %add.13), channel_id=1, source_target_pairs={{0,64},{32,96},{64,0},{96,32},{128,192},{160,224},{192,128},{224,1... | collective-permute-start | bytes 1544 | tf_op jit(solution)/shard_map/ppermute | solution.py:236
  50.2 3.5 %collective-permute-start.2 = (f32[1,128]{1,0:T(1,128)S(1)}, f32[1,128]{1,0:T(1,128)S(1)}, u32[]{:S(2)}, u32[]{:S(2)}) collective-permute-start(f32[1,128]{1,0:T(1,128)S(1)} %add.14), channel_id=1, source_target_pairs={{0,32},{32,0},{64,96},{96,64},{128,160},{160,128},{192,224},{224,1... | collective-permute-start | bytes 1544 | tf_op jit(solution)/shard_map/ppermute | solution.py:236

commit v3 on v2

--- a/solution.py
+++ b/solution.py
@@ -81,6 +81,20 @@
     )(queries, attn_keys, attn_values, byte_grads, seg_starts)
 
 
+def dot(left, right):
+    return jnp.dot(left, right, preferred_element_type=jnp.float32)
+
+
+def dot_t(left, right):
+    contract_last = (((1,), (1,)), ((), ()))
+    return lax.dot_general(left, right, contract_last, preferred_element_type=jnp.float32)
+
+
+def add_late(combine, wide, late):
+    half = late.shape[1]
+    return jnp.concatenate([wide[:, :half], combine(wide[:, half:], late)], axis=1)
+
+
 def attention_kernel(
     block,
     packed_ref,
@@ -119,42 +133,58 @@
     key_t = key.T
     value_t = value.T
     gain_grad = jnp.zeros((1, width), jnp.float32)
-    contract_last = (((1,), (1,)), ((), ()))
+    half = block // 2
+    causal = lax.broadcasted_iota(jnp.int32, (half, half), 0) <= lax.broadcasted_iota(
+        jnp.int32, (half, half), 1
+    )
     blocks = total // block
     copies = []
     for index in reversed(range(blocks)):
         first = index * block
+        middle = first + half
         prefix = first + block
         query_block = query[first:prefix]
         upstream_block = upstream_ref[first:prefix]
-        scores = lax.dot_general(
-            key[:prefix], query_block, contract_last, preferred_element_type=jnp.float32
-        )
-        bias = jnp.concatenate([bias_ref[:prefix]] * (block // width), axis=1)
-        scores = scores + bias
-        key_ids = lax.broadcasted_iota(jnp.int32, (block, block), 0)
-        query_ids = lax.broadcasted_iota(jnp.int32, (block, block), 1)
-        diagonal = jnp.where(key_ids <= query_ids, scores[first:], -1e30)
-        scores = jnp.concatenate([scores[:first], diagonal], axis=0) if first else diagonal
-        row_max = jnp.max(scores, axis=0, keepdims=True)
-        weights = jnp.exp((scores - row_max) * scaling)
-        probs = weights * (1.0 / jnp.sum(weights, axis=0, keepdims=True))
-        probs_low = probs.astype(jnp.bfloat16)
-        out_t = jnp.dot(value_t[:, :prefix], probs_low, preferred_element_type=jnp.float32)
+        wide = dot_t(key[:middle], query_block)
+        late = dot_t(key[middle:prefix], query_block[half:])
+        wide = wide + jnp.concatenate([bias_ref[:middle]] * (block // width), axis=1)
+        late = late + jnp.concatenate([bias_ref[middle:prefix]] * (half // width), axis=1)
+        late = jnp.where(causal, late, -1e30)
+        square = jnp.where(causal, wide[first:, :half], -1e30)
+        square = jnp.concatenate([square, wide[first:, half:]], axis=1)
+        wide = jnp.concatenate([wide[:first], square], axis=0) if first else square
+        row_max = add_late(
+            jnp.maximum, jnp.max(wide, axis=0, keepdims=True), jnp.max(late, axis=0, keepdims=True)
+        )
+        wide = jnp.exp((wide - row_max) * scaling)
+        late = jnp.exp((late - row_max[:, half:]) * scaling)
+        inverse = 1.0 / add_late(
+            jnp.add, jnp.sum(wide, axis=0, keepdims=True), jnp.sum(late, axis=0, keepdims=True)
+        )
+        wide_probs = wide * inverse
+        late_probs = late * inverse[:, half:]
+        wide_low = wide_probs.astype(jnp.bfloat16)
+        late_low = late_probs.astype(jnp.bfloat16)
+        out_t = add_late(
+            jnp.add, dot(value_t[:, :middle], wide_low), dot(value_t[:, middle:prefix], late_low)
+        )
         out_t = out_t.astype(jnp.bfloat16).astype(jnp.float32)
         upstream_t = upstream_block.astype(jnp.float32).T
         row_delta = jnp.sum(upstream_t * out_t, axis=0, keepdims=True)
         gain_grad += jnp.sum(
             out_t.T * pooled_ref[first:prefix].astype(jnp.float32), axis=0, keepdims=True
         )
-        grad_probs = lax.dot_general(
-            value[:prefix], upstream_block, contract_last, preferred_element_type=jnp.float32
-        )
-        grad_scores = (probs * (grad_probs - row_delta)).astype(jnp.bfloat16)
-        dq_t = jnp.dot(key_t[:, :prefix], grad_scores, preferred_element_type=jnp.float32)
-        dk = jnp.dot(grad_scores, query_block, preferred_element_type=jnp.float32)
-        dv = jnp.dot(probs_low, upstream_block, preferred_element_type=jnp.float32)
-        dk_own, dv_own = dk[first:], dv[first:]
+        wide_grad = dot_t(value[:middle], upstream_block) - row_delta
+        late_grad = dot_t(value[middle:prefix], upstream_block[half:]) - row_delta[:, half:]
+        wide_grad = (wide_probs * wide_grad).astype(jnp.bfloat16)
+        late_grad = (late_probs * late_grad).astype(jnp.bfloat16)
+        dq_t = add_late(
+            jnp.add, dot(key_t[:, :middle], wide_grad), dot(key_t[:, middle:prefix], late_grad)
+        )
+        dk = dot(wide_grad, query_block)
+        dv = dot(wide_low, upstream_block)
+        dk_own = jnp.concatenate([dk[first:], dot(late_grad, query_block[half:])], axis=0)
+        dv_own = jnp.concatenate([dv[first:], dot(late_low, upstream_block[half:])], axis=0)
         if index < blocks - 1:
             dk_own = dk_own + dk_ref[first:prefix]
             dv_own = dv_own + dv_ref[first:prefix]

time: 54.6 us -> 54.3 us (level)
  no operation moved by 1% of the time
where the time goes in v3:
time: 54.3 us; the launch traced here: 54 us
  starting transfers between devices  24.4 us (45%)
  waiting for transfers between devices  20.6 us (38%)
  Pallas kernels  7.84 us (14%)
  between operations  0.69 us (1%)
    all_to_all x1, waiting for transfers between devices, per_device(): lax.all_to_all(packed, 'seq', split_axis=0, concat_axis=0, tiled=True)  15.1 us
    ppermute x3, starting transfers between devices, group_half(): return lax.ppermute(value, 'grp', [(i, i ^ step) for i in range(count)])  10.3 us
    all_to_all x1, starting transfers between devices, per_device(): lax.all_to_all(packed, 'seq', split_axis=0, concat_axis=0, tiled=True)  7.62 us
    all_to_all x1, starting transfers between devices, per_device(): lax.all_to_all(grads, 'seq', split_axis=0, concat_axis=0, tiled=True)  6.44 us
    ppermute x3, waiting for transfers between devices, group_half(): return lax.ppermute(value, 'grp', [(i, i ^ step) for i in range(count)])  5.45 us
    pallas_call x1, Pallas kernels, attention(): pl.pallas_call(functools.partial(attention_kernel, block), in_specs=[vmem...  3.77 us
    pallas_call x1, Pallas kernels, pack(): pl.pallas_call(pack_kernel, grid=(steps,), in_specs=[slot_spec, slot_spec...  3.06 us
  transfers between devices with their start and end apart: 5, of which 4 were waited for; matrix products, arithmetic and copies ran while one was open for 0% of the time, Pallas kernels for 2%

profile of v3, /device:TPU:2, one launch (start us, length us, event | category | flops | bytes accessed | tf_op | source)
XLA Modules:
  0.0 54.0 jit_solution(11528293165673000801)
XLA Ops:
  0.6 0.0 copy-start
  0.6 3.1 %pool_and_pack.1 = bf16[32,136,128]{2,1,0:T(8,128)(2,1)} custom-call(bf16[1,32,4096]{2,1,0:T(8,128)(2,1)} %query_ref.1, bf16[1,32,4096]{2,1,0:T(8,128)(2,1)} %key_ref.1, bf16[1,32,4096]{2,1,0:T(8,128)(2,1)} %value_ref.1, bf16[1,256,4096]{2,1,0:T(8,128)(2,1)} %bytes_ref.1, s32[1,1,32]{2,1,0:T(1,128)} %starts_ref.1), custom_call_target="tpu_custom_call" | custom-call | tf_op jit(solution)/shard_map/pool_and_pack/pallas_call | solution.py:67
  3.7 7.6 %all-to-all-start = ((bf16[32,136,128]{2,1,0:T(8,128)(2,1)}), bf16[32,136,128]{2,1,0:T(8,128)(2,1)S(1)}, u32[]{:S(2)}, u32[]{:S(2)}) async-start(bf16[32,136,128]{2,1,0:T(8,128)(2,1)} %pool_and_pack.1), calls=%async_computation | async-start | bytes 2228224 | tf_op jit(solution)/shard_map/all_to_all | solution.py:271
  11.3 0.0 copy-done
  11.4 15.1 %all-to-all-done.packed_ref = bf16[32,136,128]{2,1,0:T(8,128)(2,1)S(1)} async-done(((bf16[32,136,128]{2,1,0:T(8,128)(2,1)}), bf16[32,136,128]{2,1,0:T(8,128)(2,1)S(1)}, u32[]{:S(2)}, u32[]{:S(2)}) %all-to-all-start) | async-done | bytes 1114144 | tf_op jit(solution)/shard_map/all_to_all | solution.py:271
  26.5 3.8 %attention_grads.1 = (bf16[32,96,128]{2,1,0:T(8,128)(2,1)}, f32[1,128]{1,0:T(1,128)S(1)}) custom-call(bf16[32,136,128]{2,1,0:T(8,128)(2,1)S(1)} %all-to-all-done.packed_ref, f32[1,128]{1,0:T(1,128)S(1)} %constant_dynamic-slice_fusion.gain_ref), custom_call_target="tpu_custom_call" | custom-call | tf_op jit(solution)/shard_map/attention_grads/pallas_call | solution.py:219
  30.2 6.4 %all-to-all-start.1 = ((bf16[32,96,128]{2,1,0:T(8,128)(2,1)}), bf16[32,96,128]{2,1,0:T(8,128)(2,1)S(1)}, u32[]{:S(2)}, u32[]{:S(2)}) async-start(bf16[32,96,128]{2,1,0:T(8,128)(2,1)} %get-tuple-element.11), calls=%async_computation.1 | async-start | bytes 1572864 | tf_op jit(solution)/shard_map/all_to_all | solution.py:274
  36.7 7.3 %collective-permute-start = (f32[1,128]{1,0:T(1,128)S(1)}, f32[1,128]{1,0:T(1,128)S(1)}, u32[]{:S(2)}, u32[]{:S(2)}) collective-permute-start(f32[1,128]{1,0:T(1,128)S(1)} %get-tuple-element.14), channel_id=1, source_target_pairs={{0,128},{32,160},{64,192},{96,224},{128,0},{160,32},{192,64},{224,... | collective-permute-start | bytes 1544 | tf_op jit(solution)/shard_map/ppermute | solution.py:266
  44.0 1.5 %collective-permute-done = f32[1,128]{1,0:T(1,128)S(1)} collective-permute-done((f32[1,128]{1,0:T(1,128)S(1)}, f32[1,128]{1,0:T(1,128)S(1)}, u32[]{:S(2)}, u32[]{:S(2)}) %collective-permute-start) | collective-permute-done | bytes 544 | tf_op jit(solution)/shard_map/ppermute | solution.py:266
  45.5 2.0 %collective-permute-start.1 = (f32[1,128]{1,0:T(1,128)S(1)}, f32[1,128]{1,0:T(1,128)S(1)}, u32[]{:S(2)}, u32[]{:S(2)}) collective-permute-start(f32[1,128]{1,0:T(1,128)S(1)} %add.13), channel_id=1, source_target_pairs={{0,64},{32,96},{64,0},{96,32},{128,192},{160,224},{192,128},{224,1... | collective-permute-start | bytes 1544 | tf_op jit(solution)/shard_map/ppermute | solution.py:266
  47.5 2.4 %collective-permute-done.1 = f32[1,128]{1,0:T(1,128)S(1)} collective-permute-done((f32[1,128]{1,0:T(1,128)S(1)}, f32[1,128]{1,0:T(1,128)S(1)}, u32[]{:S(2)}, u32[]{:S(2)}) %collective-permute-start.1) | collective-permute-done | bytes 544 | tf_op jit(solution)/shard_map/ppermute | solution.py:266
  49.9 1.0 %collective-permute-start.2 = (f32[1,128]{1,0:T(1,128)S(1)}, f32[1,128]{1,0:T(1,128)S(1)}, u32[]{:S(2)}, u32[]{:S(2)}) collective-permute-start(f32[1,128]{1,0:T(1,128)S(1)} %add.14), channel_id=1, source_target_pairs={{0,32},{32,0},{64,96},{96,64},{128,160},{160,128},{192,224},{224,1... | collective-permute-start | bytes 1544 | tf_op jit(solution)/shard_map/ppermute | solution.py:266
  51.0 0.0 all-to-all-done.1.grads_ref
  51.0 1.0 %unpack_grads.1 = (bf16[1,32,4096]{2,1,0:T(8,128)(2,1)}, bf16[1,32,4096]{2,1,0:T(8,128)(2,1)}, bf16[1,32,4096]{2,1,0:T(8,128)(2,1)}) custom-call(bf16[32,96,128]{2,1,0:T(8,128)(2,1)S(1)} %all-to-all-done.1.grads_ref), custom_call_target="tpu_custom_call" | custom-call | tf_op jit(solution)/shard_map/unpack_grads/pallas_call | solution.py:254
  52.0 1.5 %collective-permute-done.2 = f32[1,128]{1,0:T(1,128)S(1)} collective-permute-done((f32[1,128]{1,0:T(1,128)S(1)}, f32[1,128]{1,0:T(1,128)S(1)}, u32[]{:S(2)}, u32[]{:S(2)}) %collective-permute-start.2) | collective-permute-done | bytes 544 | tf_op jit(solution)/shard_map/ppermute | solution.py:266
  53.5 0.5 add_bitcast_fusion
  (3 shorter events, 0.0 us)
Async XLA Ops:
  0.6 10.7 %copy-start = (f32[4096]{0:T(1024)S(1)}, f32[4096]{0:T(1024)}, u32[]{:S(2)}) copy-start(f32[4096]{0:T(1024)} %param.11) | copy-start | bytes 49156
  3.7 22.8 %all-to-all-start = ((bf16[32,136,128]{2,1,0:T(8,128)(2,1)}), bf16[32,136,128]{2,1,0:T(8,128)(2,1)S(1)}, u32[]{:S(2)}, u32[]{:S(2)}) async-start(bf16[32,136,128]{2,1,0:T(8,128)(2,1)} %pool_and_pack.1), calls=%async_computation | async-start | bytes 2228224 | tf_op jit(solution)/shard_map/all_to_all | solution.py:271
  30.2 20.7 %all-to-all-start.1 = ((bf16[32,96,128]{2,1,0:T(8,128)(2,1)}), bf16[32,96,128]{2,1,0:T(8,128)(2,1)S(1)}, u32[]{:S(2)}, u32[]{:S(2)}) async-start(bf16[32,96,128]{2,1,0:T(8,128)(2,1)} %get-tuple-element.11), calls=%async_computation.1 | async-start | bytes 1572864 | tf_op jit(solution)/shard_map/all_to_all | solution.py:274
  36.7 8.8 %collective-permute-start = (f32[1,128]{1,0:T(1,128)S(1)}, f32[1,128]{1,0:T(1,128)S(1)}, u32[]{:S(2)}, u32[]{:S(2)}) collective-permute-start(f32[1,128]{1,0:T(1,128)S(1)} %get-tuple-element.14), channel_id=1, source_target_pairs={{0,128},{32,160},{64,192},{96,224},{128,0},{160,32},{192,64},{224,... | collective-permute-start | bytes 1544 | tf_op jit(solution)/shard_map/ppermute | solution.py:266
  45.5 4.4 %collective-permute-start.1 = (f32[1,128]{1,0:T(1,128)S(1)}, f32[1,128]{1,0:T(1,128)S(1)}, u32[]{:S(2)}, u32[]{:S(2)}) collective-permute-start(f32[1,128]{1,0:T(1,128)S(1)} %add.13), channel_id=1, source_target_pairs={{0,64},{32,96},{64,0},{96,32},{128,192},{160,224},{192,128},{224,1... | collective-permute-start | bytes 1544 | tf_op jit(solution)/shard_map/ppermute | solution.py:266
  49.9 3.5 %collective-permute-start.2 = (f32[1,128]{1,0:T(1,128)S(1)}, f32[1,128]{1,0:T(1,128)S(1)}, u32[]{:S(2)}, u32[]{:S(2)}) collective-permute-start(f32[1,128]{1,0:T(1,128)S(1)} %add.14), channel_id=1, source_target_pairs={{0,32},{32,0},{64,96},{96,64},{128,160},{160,128},{192,224},{224,1... | collective-permute-start | bytes 1544 | tf_op jit(solution)/shard_map/ppermute | solution.py:266

commit v4 on v3

--- a/solution.py
+++ b/solution.py
@@ -165,6 +165,27 @@
         late_probs = late * inverse[:, half:]
         wide_low = wide_probs.astype(jnp.bfloat16)
         late_low = late_probs.astype(jnp.bfloat16)
+        owners = slice(first // slots, prefix // slots)
+        shape = (block // slots, slots, width)
+
+        def send(kind, array):
+            rows = slice(kind * slots, (kind + 1) * slots)
+            staged_ref[owners, rows, :] = array.astype(jnp.bfloat16).reshape(shape)
+            copy = pltpu.make_async_copy(
+                staged_ref.at[owners, rows], grads_ref.at[owners, rows], sems.at[index, kind]
+            )
+            copy.start()
+            copies.append(copy)
+
+        dv = dot(wide_low, upstream_block)
+        dv_own = jnp.concatenate([dv[first:], dot(late_low, upstream_block[half:])], axis=0)
+        if index < blocks - 1:
+            dv_own = dv_own + dv_ref[first:prefix]
+        if first and index < blocks - 1:
+            dv_ref[:first] += dv[:first]
+        elif first:
+            dv_ref[:first] = dv[:first]
+        send(2, dv_own)
         out_t = add_late(
             jnp.add, dot(value_t[:, :middle], wide_low), dot(value_t[:, middle:prefix], late_low)
         )
@@ -181,31 +202,16 @@
         dq_t = add_late(
             jnp.add, dot(key_t[:, :middle], wide_grad), dot(key_t[:, middle:prefix], late_grad)
         )
+        send(0, dq_t.T * scaling)
         dk = dot(wide_grad, query_block)
-        dv = dot(wide_low, upstream_block)
         dk_own = jnp.concatenate([dk[first:], dot(late_grad, query_block[half:])], axis=0)
-        dv_own = jnp.concatenate([dv[first:], dot(late_low, upstream_block[half:])], axis=0)
         if index < blocks - 1:
             dk_own = dk_own + dk_ref[first:prefix]
-            dv_own = dv_own + dv_ref[first:prefix]
         if first and index < blocks - 1:
             dk_ref[:first] += dk[:first]
-            dv_ref[:first] += dv[:first]
         elif first:
             dk_ref[:first] = dk[:first]
-            dv_ref[:first] = dv[:first]
-        owners = slice(first // slots, prefix // slots)
-        shape = (block // slots, slots, width)
-        staged_ref[owners, 0:slots, :] = (dq_t.T * scaling).astype(jnp.bfloat16).reshape(shape)
-        staged_ref[owners, slots : 2 * slots, :] = (
-            (dk_own * scaling).astype(jnp.bfloat16).reshape(shape)
-        )
-        staged_ref[owners, 2 * slots :, :] = dv_own.astype(jnp.bfloat16).reshape(shape)
-        copy = pltpu.make_async_copy(
-            staged_ref.at[owners], grads_ref.at[owners], sems.at[index]
-        )
-        copy.start()
-        copies.append(copy)
+        send(1, dk_own * scaling)
     gain_grad_ref[...] = gain_grad
     for copy in copies:
         copy.wait()
@@ -231,39 +237,58 @@
             pltpu.VMEM((total, width), jnp.float32),
             pltpu.VMEM((total, width), jnp.float32),
             pltpu.VMEM((shards, 3 * slots, width), jnp.bfloat16),
-            pltpu.SemaphoreType.DMA((total // block,)),
+            pltpu.SemaphoreType.DMA((total // block, 3)),
         ],
         compiler_params=pltpu.CompilerParams(vmem_limit_bytes=40 * 2**20),
         name="attention_grads",
     )(packed, gain)
 
 
-def unpack_kernel(grads_ref, dq_ref, dk_ref, dv_ref):
+def unpack_kernel(
+    grads_ref, here_ref, other_ref, dq_ref, dk_ref, dv_ref, gain_ref, staged_ref, sum_ref, sems
+):
     slots = dq_ref.shape[1]
-    for head in range(grads_ref.shape[0]):
-        cols = slice(head * HD, (head + 1) * HD)
-        dq_ref[0, :, cols] = grads_ref[head, 0:slots, :]
-        dk_ref[0, :, cols] = grads_ref[head, slots : 2 * slots, :]
-        dv_ref[0, :, cols] = grads_ref[head, 2 * slots :, :]
-
-
-def unpack(grads):
+    sum_ref[...] = here_ref[...] + other_ref[...]
+    copies = [pltpu.make_async_copy(sum_ref, gain_ref, sems.at[3])]
+    copies[0].start()
+    for kind, out_ref in enumerate((dq_ref, dk_ref, dv_ref)):
+        for head in range(grads_ref.shape[0]):
+            cols = slice(head * HD, (head + 1) * HD)
+            rows = slice(kind * slots, (kind + 1) * slots)
+            staged_ref[kind, 0, :, cols] = grads_ref[head, rows, :]
+        copy = pltpu.make_async_copy(staged_ref.at[kind], out_ref, sems.at[kind])
+        copy.start()
+        copies.append(copy)
+    for copy in copies:
+        copy.wait()
+
+
+def unpack(grads, here, other):
     heads, rows, width = grads.shape
-    out = jax.ShapeDtypeStruct((1, rows // 3, heads * width), jnp.bfloat16)
+    shape = (1, rows // 3, heads * width)
     vmem = pl.BlockSpec(memory_space=pltpu.VMEM)
     return pl.pallas_call(
         unpack_kernel,
-        in_specs=[vmem],
-        out_specs=[vmem] * 3,
-        out_shape=[out] * 3,
+        in_specs=[vmem] * 3,
+        out_specs=[pl.BlockSpec(memory_space=pl.ANY)] * 4,
+        out_shape=[jax.ShapeDtypeStruct(shape, jnp.bfloat16)] * 3
+        + [jax.ShapeDtypeStruct((1, width), jnp.float32)],
+        scratch_shapes=[
+            pltpu.VMEM((3,) + shape, jnp.bfloat16),
+            pltpu.VMEM((1, width), jnp.float32),
+            pltpu.SemaphoreType.DMA((4,)),
+        ],
         compiler_params=pltpu.CompilerParams(vmem_limit_bytes=16 * 2**20),
         name="unpack_grads",
-    )(grads)
-
-
-def group_half(value, step):
+    )(grads, here, other)
+
+
+RING_STEPS = (1, 7, 2)
+
+
+def group_half(value, mask):
     count = lax.axis_size("grp")
-    return lax.ppermute(value, "grp", [(i, i ^ step) for i in range(count)])
+    return lax.ppermute(value, "grp", [(i, i ^ mask) for i in range(count)])
 
 
 def per_device(queries, attn_keys, attn_values, byte_grads, seg_starts, up_gain):
@@ -272,14 +297,11 @@
     gain = lax.dynamic_slice_in_dim(up_gain.reshape(-1, HD), lax.axis_index("seq"), 1)
     grads, gain_grad = attention(received, gain, 512)
     returned = lax.all_to_all(grads, "seq", split_axis=0, concat_axis=0, tiled=True)
-    step = lax.axis_size("grp") // 2
-    while step > 1:
-        gain_grad = gain_grad + group_half(gain_grad, step)
-        step //= 2
-    other = group_half(gain_grad, step)
-    dq, dk, dv = unpack(returned)
-    gain_grad, dv = lax.optimization_barrier((gain_grad, dv))
-    return dq, dk, dv, (gain_grad + other).reshape(HD)
+    for mask in RING_STEPS[:-1]:
+        gain_grad = gain_grad + group_half(gain_grad, mask)
+    other = group_half(gain_grad, RING_STEPS[-1])
+    dq, dk, dv, gain_grad = unpack(returned, gain_grad, other)
+    return dq, dk, dv, gain_grad.reshape(HD)
 
 
 def solution(mesh):

time: 54.3 us -> 53.3 us (0.982)
  transfers between devices with their start and end apart: 5 -> 5, of which waited for: 4 -> 4; matrix products, arithmetic and copies ran while one was open for 0% -> 0% of each run, Pallas kernels for 2% -> 0%
where the time goes in v4:
time: 53.3 us; the launch traced here: 52.9 us
  starting transfers between devices  24.4 us (46%)
  waiting for transfers between devices  20.2 us (38%)
  Pallas kernels  7.61 us (14%)
  between operations  0.69 us (1%)
    all_to_all x1, waiting for transfers between devices, per_device(): lax.all_to_all(packed, 'seq', split_axis=0, concat_axis=0, tiled=True)  15.1 us
    ppermute x3, starting transfers between devices, group_half(): return lax.ppermute(value, 'grp', [(i, i ^ mask) for i in range(count)])  10.3 us
    all_to_all x1, starting transfers between devices, per_device(): lax.all_to_all(packed, 'seq', split_axis=0, concat_axis=0, tiled=True)  7.62 us
    all_to_all x1, starting transfers between devices, per_device(): lax.all_to_all(grads, 'seq', split_axis=0, concat_axis=0, tiled=True)  6.44 us
    ppermute x3, waiting for transfers between devices, group_half(): return lax.ppermute(value, 'grp', [(i, i ^ mask) for i in range(count)])  5.14 us
    pallas_call x1, Pallas kernels, attention(): pl.pallas_call(functools.partial(attention_kernel, block), in_specs=[vmem...  3.6 us
    pallas_call x1, Pallas kernels, pack(): pl.pallas_call(pack_kernel, grid=(steps,), in_specs=[slot_spec, slot_spec...  3.06 us
  transfers between devices with their start and end apart: 5, of which 4 were waited for; matrix products, arithmetic and copies ran while one was open for 0% of the time, Pallas kernels for 0%

profile of v4, /device:TPU:2, one launch (start us, length us, event | category | flops | bytes accessed | tf_op | source)
XLA Modules:
  0.0 52.9 jit_solution(6945876743650030629)
XLA Ops:
  0.6 0.0 copy-start
  0.6 3.1 %pool_and_pack.1 = bf16[32,136,128]{2,1,0:T(8,128)(2,1)} custom-call(bf16[1,32,4096]{2,1,0:T(8,128)(2,1)} %query_ref.1, bf16[1,32,4096]{2,1,0:T(8,128)(2,1)} %key_ref.1, bf16[1,32,4096]{2,1,0:T(8,128)(2,1)} %value_ref.1, bf16[1,256,4096]{2,1,0:T(8,128)(2,1)} %bytes_ref.1, s32[1,1,32]{2,1,0:T(1,128)} %starts_ref.1), custom_call_target="tpu_custom_call" | custom-call | tf_op jit(solution)/shard_map/pool_and_pack/pallas_call | solution.py:67
  3.7 7.6 %all-to-all-start = ((bf16[32,136,128]{2,1,0:T(8,128)(2,1)}), bf16[32,136,128]{2,1,0:T(8,128)(2,1)S(1)}, u32[]{:S(2)}, u32[]{:S(2)}) async-start(bf16[32,136,128]{2,1,0:T(8,128)(2,1)} %pool_and_pack.1), calls=%async_computation | async-start | bytes 2228224 | tf_op jit(solution)/shard_map/all_to_all | solution.py:296
  11.3 0.0 copy-done
  11.4 15.1 %all-to-all-done.packed_ref = bf16[32,136,128]{2,1,0:T(8,128)(2,1)S(1)} async-done(((bf16[32,136,128]{2,1,0:T(8,128)(2,1)}), bf16[32,136,128]{2,1,0:T(8,128)(2,1)S(1)}, u32[]{:S(2)}, u32[]{:S(2)}) %all-to-all-start) | async-done | bytes 1114144 | tf_op jit(solution)/shard_map/all_to_all | solution.py:296
  26.5 3.6 %attention_grads.1 = (bf16[32,96,128]{2,1,0:T(8,128)(2,1)}, f32[1,128]{1,0:T(1,128)S(1)}) custom-call(bf16[32,136,128]{2,1,0:T(8,128)(2,1)S(1)} %all-to-all-done.packed_ref, f32[1,128]{1,0:T(1,128)S(1)} %constant_dynamic-slice_fusion.gain_ref), custom_call_target="tpu_custom_call" | custom-call | tf_op jit(solution)/shard_map/attention_grads/pallas_call | solution.py:225
  30.1 6.4 %all-to-all-start.1 = ((bf16[32,96,128]{2,1,0:T(8,128)(2,1)}), bf16[32,96,128]{2,1,0:T(8,128)(2,1)S(1)}, u32[]{:S(2)}, u32[]{:S(2)}) async-start(bf16[32,96,128]{2,1,0:T(8,128)(2,1)} %get-tuple-element.10), calls=%async_computation.1 | async-start | bytes 1572864 | tf_op jit(solution)/shard_map/all_to_all | solution.py:299
  36.5 2.0 %collective-permute-start = (f32[1,128]{1,0:T(1,128)S(1)}, f32[1,128]{1,0:T(1,128)S(1)}, u32[]{:S(2)}, u32[]{:S(2)}) collective-permute-start(f32[1,128]{1,0:T(1,128)S(1)} %get-tuple-element.11), channel_id=1, source_target_pairs={{0,32},{32,0},{64,96},{96,64},{128,160},{160,128},{192,224},{224,1... | collective-permute-start | bytes 1544 | tf_op jit(solution)/shard_map/ppermute | solution.py:291
  38.5 1.6 %collective-permute-done = f32[1,128]{1,0:T(1,128)S(1)} collective-permute-done((f32[1,128]{1,0:T(1,128)S(1)}, f32[1,128]{1,0:T(1,128)S(1)}, u32[]{:S(2)}, u32[]{:S(2)}) %collective-permute-start) | collective-permute-done | bytes 544 | tf_op jit(solution)/shard_map/ppermute | solution.py:291
  40.2 5.9 %collective-permute-start.1 = (f32[1,128]{1,0:T(1,128)S(1)}, f32[1,128]{1,0:T(1,128)S(1)}, u32[]{:S(2)}, u32[]{:S(2)}) collective-permute-start(f32[1,128]{1,0:T(1,128)S(1)} %add.10), channel_id=1, source_target_pairs={{0,224},{32,192},{64,160},{96,128},{128,96},{160,64},{192,32},{224... | collective-permute-start | bytes 1544 | tf_op jit(solution)/shard_map/ppermute | solution.py:291
  46.0 1.5 %collective-permute-done.1 = f32[1,128]{1,0:T(1,128)S(1)} collective-permute-done((f32[1,128]{1,0:T(1,128)S(1)}, f32[1,128]{1,0:T(1,128)S(1)}, u32[]{:S(2)}, u32[]{:S(2)}) %collective-permute-start.1) | collective-permute-done | bytes 544 | tf_op jit(solution)/shard_map/ppermute | solution.py:291
  47.5 2.4 %collective-permute-start.2 = (f32[1,128]{1,0:T(1,128)S(1)}, f32[1,128]{1,0:T(1,128)S(1)}, u32[]{:S(2)}, u32[]{:S(2)}) collective-permute-start(f32[1,128]{1,0:T(1,128)S(1)} %add.11.here_ref), channel_id=1, source_target_pairs={{0,64},{32,96},{64,0},{96,32},{128,192},{160,224},{192,128},{224,1... | collective-permute-start | bytes 1544 | tf_op jit(solution)/shard_map/ppermute | solution.py:291
  50.0 2.0 %collective-permute-done.2.other_ref = f32[1,128]{1,0:T(1,128)S(1)} collective-permute-done((f32[1,128]{1,0:T(1,128)S(1)}, f32[1,128]{1,0:T(1,128)S(1)}, u32[]{:S(2)}, u32[]{:S(2)}) %collective-permute-start.2) | collective-permute-done | bytes 544 | tf_op jit(solution)/shard_map/ppermute | solution.py:291
  52.0 0.0 all-to-all-done.1.grads_ref
  52.0 1.0 %unpack_grads.1 = (bf16[1,32,4096]{2,1,0:T(8,128)(2,1)}, bf16[1,32,4096]{2,1,0:T(8,128)(2,1)}, bf16[1,32,4096]{2,1,0:T(8,128)(2,1)}, f32[1,128]{1,0:T(1,128)}) custom-call(bf16[32,96,128]{2,1,0:T(8,128)(2,1)S(1)} %all-to-all-done.1.grads_ref, f32[1,128]{1,0:T(1,128)S(1)} %add.11.here_ref, f32[1,128]{1,0:T(1,128)S(1)} %collective-permute-done.2.other_ref), custom_call_target="tpu_custom_call" | custom-call | tf_op jit(solution)/shard_map/unpack_grads/pallas_call | solution.py:270
  (3 shorter events, 0.0 us)
Async XLA Ops:
  0.6 10.7 %copy-start = (f32[4096]{0:T(1024)S(1)}, f32[4096]{0:T(1024)}, u32[]{:S(2)}) copy-start(f32[4096]{0:T(1024)} %param.11) | copy-start | bytes 49156
  3.7 22.8 %all-to-all-start = ((bf16[32,136,128]{2,1,0:T(8,128)(2,1)}), bf16[32,136,128]{2,1,0:T(8,128)(2,1)S(1)}, u32[]{:S(2)}, u32[]{:S(2)}) async-start(bf16[32,136,128]{2,1,0:T(8,128)(2,1)} %pool_and_pack.1), calls=%async_computation | async-start | bytes 2228224 | tf_op jit(solution)/shard_map/all_to_all | solution.py:296
  30.1 21.9 %all-to-all-start.1 = ((bf16[32,96,128]{2,1,0:T(8,128)(2,1)}), bf16[32,96,128]{2,1,0:T(8,128)(2,1)S(1)}, u32[]{:S(2)}, u32[]{:S(2)}) async-start(bf16[32,96,128]{2,1,0:T(8,128)(2,1)} %get-tuple-element.10), calls=%async_computation.1 | async-start | bytes 1572864 | tf_op jit(solution)/shard_map/all_to_all | solution.py:299
  36.5 3.6 %collective-permute-start = (f32[1,128]{1,0:T(1,128)S(1)}, f32[1,128]{1,0:T(1,128)S(1)}, u32[]{:S(2)}, u32[]{:S(2)}) collective-permute-start(f32[1,128]{1,0:T(1,128)S(1)} %get-tuple-element.11), channel_id=1, source_target_pairs={{0,32},{32,0},{64,96},{96,64},{128,160},{160,128},{192,224},{224,1... | collective-permute-start | bytes 1544 | tf_op jit(solution)/shard_map/ppermute | solution.py:291
  40.2 7.4 %collective-permute-start.1 = (f32[1,128]{1,0:T(1,128)S(1)}, f32[1,128]{1,0:T(1,128)S(1)}, u32[]{:S(2)}, u32[]{:S(2)}) collective-permute-start(f32[1,128]{1,0:T(1,128)S(1)} %add.10), channel_id=1, source_target_pairs={{0,224},{32,192},{64,160},{96,128},{128,96},{160,64},{192,32},{224... | collective-permute-start | bytes 1544 | tf_op jit(solution)/shard_map/ppermute | solution.py:291
  47.5 4.4 %collective-permute-start.2 = (f32[1,128]{1,0:T(1,128)S(1)}, f32[1,128]{1,0:T(1,128)S(1)}, u32[]{:S(2)}, u32[]{:S(2)}) collective-permute-start(f32[1,128]{1,0:T(1,128)S(1)} %add.11.here_ref), channel_id=1, source_target_pairs={{0,64},{32,96},{64,0},{96,32},{128,192},{160,224},{192,128},{224,1... | collective-permute-start | bytes 1544 | tf_op jit(solution)/shard_map/ppermute | solution.py:291

commit v5 on v4

--- a/solution.py
+++ b/solution.py
@@ -90,13 +90,16 @@
     return lax.dot_general(left, right, contract_last, preferred_element_type=jnp.float32)
 
 
-def add_late(combine, wide, late):
-    half = late.shape[1]
-    return jnp.concatenate([wide[:, :half], combine(wide[:, half:], late)], axis=1)
+def joined(combine, parts):
+    whole = parts[0]
+    for part in parts[1:]:
+        first = whole.shape[1] - part.shape[1]
+        whole = jnp.concatenate([whole[:, :first], combine(whole[:, first:], part)], axis=1)
+    return whole
 
 
 def attention_kernel(
-    block,
+    band,
     packed_ref,
     gain_ref,
     grads_ref,
@@ -104,8 +107,6 @@
     upstream_ref,
     pooled_ref,
     bias_ref,
-    dk_ref,
-    dv_ref,
     staged_ref,
     sems,
 ):
@@ -132,98 +133,73 @@
     value = packed_ref[:, 2 * slots : 3 * slots, :].reshape(total, width)
     key_t = key.T
     value_t = value.T
-    gain_grad = jnp.zeros((1, width), jnp.float32)
-    half = block // 2
-    causal = lax.broadcasted_iota(jnp.int32, (half, half), 0) <= lax.broadcasted_iota(
-        jnp.int32, (half, half), 1
-    )
-    blocks = total // block
+    causal = lax.broadcasted_iota(jnp.int32, (band, band), 0) <= lax.broadcasted_iota(
+        jnp.int32, (band, band), 1
+    )
+    upstream = upstream_ref[...]
+    starts = range(0, total, band)
     copies = []
-    for index in reversed(range(blocks)):
-        first = index * block
-        middle = first + half
-        prefix = first + block
-        query_block = query[first:prefix]
-        upstream_block = upstream_ref[first:prefix]
-        wide = dot_t(key[:middle], query_block)
-        late = dot_t(key[middle:prefix], query_block[half:])
-        wide = wide + jnp.concatenate([bias_ref[:middle]] * (block // width), axis=1)
-        late = late + jnp.concatenate([bias_ref[middle:prefix]] * (half // width), axis=1)
-        late = jnp.where(causal, late, -1e30)
-        square = jnp.where(causal, wide[first:, :half], -1e30)
-        square = jnp.concatenate([square, wide[first:, half:]], axis=1)
-        wide = jnp.concatenate([wide[:first], square], axis=0) if first else square
-        row_max = add_late(
-            jnp.maximum, jnp.max(wide, axis=0, keepdims=True), jnp.max(late, axis=0, keepdims=True)
+
+    def send(kind, first, array):
+        owners = slice(first // slots, (first + band) // slots)
+        rows = slice(kind * slots, (kind + 1) * slots)
+        staged_ref[owners, rows, :] = array.astype(jnp.bfloat16).reshape(-1, slots, width)
+        copy = pltpu.make_async_copy(
+            staged_ref.at[owners, rows], grads_ref.at[owners, rows], sems.at[first // band, kind]
         )
-        wide = jnp.exp((wide - row_max) * scaling)
-        late = jnp.exp((late - row_max[:, half:]) * scaling)
-        inverse = 1.0 / add_late(
-            jnp.add, jnp.sum(wide, axis=0, keepdims=True), jnp.sum(late, axis=0, keepdims=True)
-        )
-        wide_probs = wide * inverse
-        late_probs = late * inverse[:, half:]
-        wide_low = wide_probs.astype(jnp.bfloat16)
-        late_low = late_probs.astype(jnp.bfloat16)
-        owners = slice(first // slots, prefix // slots)
-        shape = (block // slots, slots, width)
-
-        def send(kind, array):
-            rows = slice(kind * slots, (kind + 1) * slots)
-            staged_ref[owners, rows, :] = array.astype(jnp.bfloat16).reshape(shape)
-            copy = pltpu.make_async_copy(
-                staged_ref.at[owners, rows], grads_ref.at[owners, rows], sems.at[index, kind]
-            )
-            copy.start()
-            copies.append(copy)
-
-        dv = dot(wide_low, upstream_block)
-        dv_own = jnp.concatenate([dv[first:], dot(late_low, upstream_block[half:])], axis=0)
-        if index < blocks - 1:
-            dv_own = dv_own + dv_ref[first:prefix]
-        if first and index < blocks - 1:
-            dv_ref[:first] += dv[:first]
-        elif first:
-            dv_ref[:first] = dv[:first]
-        send(2, dv_own)
-        out_t = add_late(
-            jnp.add, dot(value_t[:, :middle], wide_low), dot(value_t[:, middle:prefix], late_low)
-        )
-        out_t = out_t.astype(jnp.bfloat16).astype(jnp.float32)
-        upstream_t = upstream_block.astype(jnp.float32).T
-        row_delta = jnp.sum(upstream_t * out_t, axis=0, keepdims=True)
-        gain_grad += jnp.sum(
-            out_t.T * pooled_ref[first:prefix].astype(jnp.float32), axis=0, keepdims=True
-        )
-        wide_grad = dot_t(value[:middle], upstream_block) - row_delta
-        late_grad = dot_t(value[middle:prefix], upstream_block[half:]) - row_delta[:, half:]
-        wide_grad = (wide_probs * wide_grad).astype(jnp.bfloat16)
-        late_grad = (late_probs * late_grad).astype(jnp.bfloat16)
-        dq_t = add_late(
-            jnp.add, dot(key_t[:, :middle], wide_grad), dot(key_t[:, middle:prefix], late_grad)
-        )
-        send(0, dq_t.T * scaling)
-        dk = dot(wide_grad, query_block)
-        dk_own = jnp.concatenate([dk[first:], dot(late_grad, query_block[half:])], axis=0)
-        if index < blocks - 1:
-            dk_own = dk_own + dk_ref[first:prefix]
-        if first and index < blocks - 1:
-            dk_ref[:first] += dk[:first]
-        elif first:
-            dk_ref[:first] = dk[:first]
-        send(1, dk_own * scaling)
-    gain_grad_ref[...] = gain_grad
+        copy.start()
+        copies.append(copy)
+
+    scores = []
+    for first in starts:
+        part = dot_t(key[first : first + band], query[first:])
+        bias = bias_ref[first : first + band]
+        part = part + jnp.concatenate([bias] * ((total - first) // width), axis=1)
+        square = jnp.where(causal, part[:, :band], -1e30)
+        if first + band < total:
+            square = jnp.concatenate([square, part[:, band:]], axis=1)
+        scores.append(square)
+    grad_probs = [dot_t(value[i : i + band], upstream[i:]) for i in starts]
+    row_max = joined(jnp.maximum, [jnp.max(part, axis=0, keepdims=True) for part in scores])
+    weights = [
+        jnp.exp((part - row_max[:, first:]) * scaling) for first, part in zip(starts, scores)
+    ]
+    inverse = 1.0 / joined(jnp.add, [jnp.sum(part, axis=0, keepdims=True) for part in weights])
+    probs = [part * inverse[:, first:] for first, part in zip(starts, weights)]
+    probs_low = [part.astype(jnp.bfloat16) for part in probs]
+    out_t = joined(
+        jnp.add,
+        [dot(value_t[:, i : i + band], part) for i, part in zip(starts, probs_low)],
+    )
+    for first, part in zip(starts, probs_low):
+        send(2, first, dot(part, upstream[first:]))
+    out_t = out_t.astype(jnp.bfloat16).astype(jnp.float32)
+    row_delta = jnp.sum(upstream.astype(jnp.float32).T * out_t, axis=0, keepdims=True)
+    gain_grad_ref[...] = jnp.sum(
+        out_t.T * pooled_ref[...].astype(jnp.float32), axis=0, keepdims=True
+    )
+    grads = []
+    for first, part, grad in zip(starts, probs, grad_probs):
+        grads.append((part * (grad - row_delta[:, first:])).astype(jnp.bfloat16))
+    dq_t = joined(
+        jnp.add, [dot(key_t[:, i : i + band], part) for i, part in zip(starts, grads)]
+    )
+    dq = dq_t.T * scaling
+    for first in starts:
+        send(0, first, dq[first : first + band])
+    for first, part in zip(starts, grads):
+        send(1, first, dot(part, query[first:]) * scaling)
     for copy in copies:
         copy.wait()
 
 
-def attention(packed, gain, block):
+def attention(packed, gain, band):
     shards, rows, width = packed.shape
     slots = (rows - EXTRA) // 4
     total = shards * slots
     vmem = pl.BlockSpec(memory_space=pltpu.VMEM)
     return pl.pallas_call(
-        functools.partial(attention_kernel, block),
+        functools.partial(attention_kernel, band),
         in_specs=[vmem, vmem],
         out_specs=[pl.BlockSpec(memory_space=pl.ANY), vmem],
         out_shape=[
@@ -234,10 +210,8 @@
             pltpu.VMEM((total, width), jnp.bfloat16),
             pltpu.VMEM((total, width), jnp.bfloat16),
             pltpu.VMEM((total, width), jnp.float32),
-            pltpu.VMEM((total, width), jnp.float32),
-            pltpu.VMEM((total, width), jnp.float32),
             pltpu.VMEM((shards, 3 * slots, width), jnp.bfloat16),
-            pltpu.SemaphoreType.DMA((total // block, 3)),
+            pltpu.SemaphoreType.DMA((total // band, 3)),
         ],
         compiler_params=pltpu.CompilerParams(vmem_limit_bytes=40 * 2**20),
         name="attention_grads",
@@ -295,7 +269,7 @@
     packed = pack(queries, attn_keys, attn_values, byte_grads, seg_starts, 2)
     received = lax.all_to_all(packed, "seq", split_axis=0, concat_axis=0, tiled=True)
     gain = lax.dynamic_slice_in_dim(up_gain.reshape(-1, HD), lax.axis_index("seq"), 1)
-    grads, gain_grad = attention(received, gain, 512)
+    grads, gain_grad = attention(received, gain, 256)
     returned = lax.all_to_all(grads, "seq", split_axis=0, concat_axis=0, tiled=True)
     for mask in RING_STEPS[:-1]:
         gain_grad = gain_grad + group_half(gain_grad, mask)

time: 53.3 us -> 53.2 us (level)
  no operation moved by 1% of the time
where the time goes in v5:
time: 53.2 us; the launch traced here: 52.9 us
  starting transfers between devices  24.4 us (46%)
  waiting for transfers between devices  20.3 us (38%)
  Pallas kernels  7.6 us (14%)
  between operations  0.69 us (1%)
    all_to_all x1, waiting for transfers between devices, per_device(): lax.all_to_all(packed, 'seq', split_axis=0, concat_axis=0, tiled=True)  15.1 us
    ppermute x3, starting transfers between devices, group_half(): return lax.ppermute(value, 'grp', [(i, i ^ mask) for i in range(count)])  10.3 us
    all_to_all x1, starting transfers between devices, per_device(): lax.all_to_all(packed, 'seq', split_axis=0, concat_axis=0, tiled=True)  7.62 us
    all_to_all x1, starting transfers between devices, per_device(): lax.all_to_all(grads, 'seq', split_axis=0, concat_axis=0, tiled=True)  6.44 us
    ppermute x3, waiting for transfers between devices, group_half(): return lax.ppermute(value, 'grp', [(i, i ^ mask) for i in range(count)])  5.14 us
    pallas_call x1, Pallas kernels, attention(): pl.pallas_call(functools.partial(attention_kernel, band), in_specs=[vmem,...  3.59 us
    pallas_call x1, Pallas kernels, pack(): pl.pallas_call(pack_kernel, grid=(steps,), in_specs=[slot_spec, slot_spec...  3.06 us
  transfers between devices with their start and end apart: 5, of which 4 were waited for; matrix products, arithmetic and copies ran while one was open for 0% of the time, Pallas kernels for 0%

profile of v5, /device:TPU:2, one launch (start us, length us, event | category | flops | bytes accessed | tf_op | source)
XLA Modules:
  0.0 52.9 jit_solution(318382758138454429)
XLA Ops:
  0.6 0.0 copy-start
  0.6 3.1 %pool_and_pack.1 = bf16[32,136,128]{2,1,0:T(8,128)(2,1)} custom-call(bf16[1,32,4096]{2,1,0:T(8,128)(2,1)} %query_ref.1, bf16[1,32,4096]{2,1,0:T(8,128)(2,1)} %key_ref.1, bf16[1,32,4096]{2,1,0:T(8,128)(2,1)} %value_ref.1, bf16[1,256,4096]{2,1,0:T(8,128)(2,1)} %bytes_ref.1, s32[1,1,32]{2,1,0:T(1,128)} %starts_ref.1), custom_call_target="tpu_custom_call" | custom-call | tf_op jit(solution)/shard_map/pool_and_pack/pallas_call | solution.py:67
  3.7 7.6 %all-to-all-start = ((bf16[32,136,128]{2,1,0:T(8,128)(2,1)}), bf16[32,136,128]{2,1,0:T(8,128)(2,1)S(1)}, u32[]{:S(2)}, u32[]{:S(2)}) async-start(bf16[32,136,128]{2,1,0:T(8,128)(2,1)} %pool_and_pack.1), calls=%async_computation | async-start | bytes 2228224 | tf_op jit(solution)/shard_map/all_to_all | solution.py:270
  11.3 0.0 copy-done
  11.4 15.1 %all-to-all-done.packed_ref = bf16[32,136,128]{2,1,0:T(8,128)(2,1)S(1)} async-done(((bf16[32,136,128]{2,1,0:T(8,128)(2,1)}), bf16[32,136,128]{2,1,0:T(8,128)(2,1)S(1)}, u32[]{:S(2)}, u32[]{:S(2)}) %all-to-all-start) | async-done | bytes 1114144 | tf_op jit(solution)/shard_map/all_to_all | solution.py:270
  26.5 3.6 %attention_grads.1 = (bf16[32,96,128]{2,1,0:T(8,128)(2,1)}, f32[1,128]{1,0:T(1,128)S(1)}) custom-call(bf16[32,136,128]{2,1,0:T(8,128)(2,1)S(1)} %all-to-all-done.packed_ref, f32[1,128]{1,0:T(1,128)S(1)} %constant_dynamic-slice_fusion.gain_ref), custom_call_target="tpu_custom_call" | custom-call | tf_op jit(solution)/shard_map/attention_grads/pallas_call | solution.py:201
  30.1 6.4 %all-to-all-start.1 = ((bf16[32,96,128]{2,1,0:T(8,128)(2,1)}), bf16[32,96,128]{2,1,0:T(8,128)(2,1)S(1)}, u32[]{:S(2)}, u32[]{:S(2)}) async-start(bf16[32,96,128]{2,1,0:T(8,128)(2,1)} %get-tuple-element.10), calls=%async_computation.1 | async-start | bytes 1572864 | tf_op jit(solution)/shard_map/all_to_all | solution.py:273
  36.5 2.0 %collective-permute-start = (f32[1,128]{1,0:T(1,128)S(1)}, f32[1,128]{1,0:T(1,128)S(1)}, u32[]{:S(2)}, u32[]{:S(2)}) collective-permute-start(f32[1,128]{1,0:T(1,128)S(1)} %get-tuple-element.11), channel_id=1, source_target_pairs={{0,32},{32,0},{64,96},{96,64},{128,160},{160,128},{192,224},{224,1... | collective-permute-start | bytes 1544 | tf_op jit(solution)/shard_map/ppermute | solution.py:265
  38.5 1.6 %collective-permute-done = f32[1,128]{1,0:T(1,128)S(1)} collective-permute-done((f32[1,128]{1,0:T(1,128)S(1)}, f32[1,128]{1,0:T(1,128)S(1)}, u32[]{:S(2)}, u32[]{:S(2)}) %collective-permute-start) | collective-permute-done | bytes 544 | tf_op jit(solution)/shard_map/ppermute | solution.py:265
  40.2 5.9 %collective-permute-start.1 = (f32[1,128]{1,0:T(1,128)S(1)}, f32[1,128]{1,0:T(1,128)S(1)}, u32[]{:S(2)}, u32[]{:S(2)}) collective-permute-start(f32[1,128]{1,0:T(1,128)S(1)} %add.10), channel_id=1, source_target_pairs={{0,224},{32,192},{64,160},{96,128},{128,96},{160,64},{192,32},{224... | collective-permute-start | bytes 1544 | tf_op jit(solution)/shard_map/ppermute | solution.py:265
  46.0 1.5 %collective-permute-done.1 = f32[1,128]{1,0:T(1,128)S(1)} collective-permute-done((f32[1,128]{1,0:T(1,128)S(1)}, f32[1,128]{1,0:T(1,128)S(1)}, u32[]{:S(2)}, u32[]{:S(2)}) %collective-permute-start.1) | collective-permute-done | bytes 544 | tf_op jit(solution)/shard_map/ppermute | solution.py:265
  47.5 2.4 %collective-permute-start.2 = (f32[1,128]{1,0:T(1,128)S(1)}, f32[1,128]{1,0:T(1,128)S(1)}, u32[]{:S(2)}, u32[]{:S(2)}) collective-permute-start(f32[1,128]{1,0:T(1,128)S(1)} %add.11.here_ref), channel_id=1, source_target_pairs={{0,64},{32,96},{64,0},{96,32},{128,192},{160,224},{192,128},{224,1... | collective-permute-start | bytes 1544 | tf_op jit(solution)/shard_map/ppermute | solution.py:265
  50.0 2.0 %collective-permute-done.2.other_ref = f32[1,128]{1,0:T(1,128)S(1)} collective-permute-done((f32[1,128]{1,0:T(1,128)S(1)}, f32[1,128]{1,0:T(1,128)S(1)}, u32[]{:S(2)}, u32[]{:S(2)}) %collective-permute-start.2) | collective-permute-done | bytes 544 | tf_op jit(solution)/shard_map/ppermute | solution.py:265
  52.0 0.0 all-to-all-done.1.grads_ref
  52.0 1.0 %unpack_grads.1 = (bf16[1,32,4096]{2,1,0:T(8,128)(2,1)}, bf16[1,32,4096]{2,1,0:T(8,128)(2,1)}, bf16[1,32,4096]{2,1,0:T(8,128)(2,1)}, f32[1,128]{1,0:T(1,128)}) custom-call(bf16[32,96,128]{2,1,0:T(8,128)(2,1)S(1)} %all-to-all-done.1.grads_ref, f32[1,128]{1,0:T(1,128)S(1)} %add.11.here_ref, f32[1,128]{1,0:T(1,128)S(1)} %collective-permute-done.2.other_ref), custom_call_target="tpu_custom_call" | custom-call | tf_op jit(solution)/shard_map/unpack_grads/pallas_call | solution.py:244
  (3 shorter events, 0.0 us)
Async XLA Ops:
  0.6 10.7 %copy-start = (f32[4096]{0:T(1024)S(1)}, f32[4096]{0:T(1024)}, u32[]{:S(2)}) copy-start(f32[4096]{0:T(1024)} %param.11) | copy-start | bytes 49156
  3.7 22.8 %all-to-all-start = ((bf16[32,136,128]{2,1,0:T(8,128)(2,1)}), bf16[32,136,128]{2,1,0:T(8,128)(2,1)S(1)}, u32[]{:S(2)}, u32[]{:S(2)}) async-start(bf16[32,136,128]{2,1,0:T(8,128)(2,1)} %pool_and_pack.1), calls=%async_computation | async-start | bytes 2228224 | tf_op jit(solution)/shard_map/all_to_all | solution.py:270
  30.1 21.9 %all-to-all-start.1 = ((bf16[32,96,128]{2,1,0:T(8,128)(2,1)}), bf16[32,96,128]{2,1,0:T(8,128)(2,1)S(1)}, u32[]{:S(2)}, u32[]{:S(2)}) async-start(bf16[32,96,128]{2,1,0:T(8,128)(2,1)} %get-tuple-element.10), calls=%async_computation.1 | async-start | bytes 1572864 | tf_op jit(solution)/shard_map/all_to_all | solution.py:273
  36.5 3.6 %collective-permute-start = (f32[1,128]{1,0:T(1,128)S(1)}, f32[1,128]{1,0:T(1,128)S(1)}, u32[]{:S(2)}, u32[]{:S(2)}) collective-permute-start(f32[1,128]{1,0:T(1,128)S(1)} %get-tuple-element.11), channel_id=1, source_target_pairs={{0,32},{32,0},{64,96},{96,64},{128,160},{160,128},{192,224},{224,1... | collective-permute-start | bytes 1544 | tf_op jit(solution)/shard_map/ppermute | solution.py:265
  40.2 7.4 %collective-permute-start.1 = (f32[1,128]{1,0:T(1,128)S(1)}, f32[1,128]{1,0:T(1,128)S(1)}, u32[]{:S(2)}, u32[]{:S(2)}) collective-permute-start(f32[1,128]{1,0:T(1,128)S(1)} %add.10), channel_id=1, source_target_pairs={{0,224},{32,192},{64,160},{96,128},{128,96},{160,64},{192,32},{224... | collective-permute-start | bytes 1544 | tf_op jit(solution)/shard_map/ppermute | solution.py:265
  47.5 4.4 %collective-permute-start.2 = (f32[1,128]{1,0:T(1,128)S(1)}, f32[1,128]{1,0:T(1,128)S(1)}, u32[]{:S(2)}, u32[]{:S(2)}) collective-permute-start(f32[1,128]{1,0:T(1,128)S(1)} %add.11.here_ref), channel_id=1, source_target_pairs={{0,64},{32,96},{64,0},{96,32},{128,192},{160,224},{192,128},{224,1... | collective-permute-start | bytes 1544 | tf_op jit(solution)/shard_map/ppermute | solution.py:265

commit v6 on v5

--- a/solution.py
+++ b/solution.py
@@ -269,7 +269,7 @@
     packed = pack(queries, attn_keys, attn_values, byte_grads, seg_starts, 2)
     received = lax.all_to_all(packed, "seq", split_axis=0, concat_axis=0, tiled=True)
     gain = lax.dynamic_slice_in_dim(up_gain.reshape(-1, HD), lax.axis_index("seq"), 1)
-    grads, gain_grad = attention(received, gain, 256)
+    grads, gain_grad = attention(received, gain, 128)
     returned = lax.all_to_all(grads, "seq", split_axis=0, concat_axis=0, tiled=True)
     for mask in RING_STEPS[:-1]:
         gain_grad = gain_grad + group_half(gain_grad, mask)

time: 53.2 us -> 53.5 us (level)
  no operation moved by 1% of the time
where the time goes in v6:
time: 53.5 us; the launch traced here: 53.2 us
  starting transfers between devices  24.4 us (46%)
  waiting for transfers between devices  20.2 us (38%)
  Pallas kernels  7.85 us (15%)
  between operations  0.69 us (1%)
    all_to_all x1, waiting for transfers between devices, per_device(): lax.all_to_all(packed, 'seq', split_axis=0, concat_axis=0, tiled=True)  15.1 us
    ppermute x3, starting transfers between devices, group_half(): return lax.ppermute(value, 'grp', [(i, i ^ mask) for i in range(count)])  10.3 us
    all_to_all x1, starting transfers between devices, per_device(): lax.all_to_all(packed, 'seq', split_axis=0, concat_axis=0, tiled=True)  7.62 us
    all_to_all x1, starting transfers between devices, per_device(): lax.all_to_all(grads, 'seq', split_axis=0, concat_axis=0, tiled=True)  6.43 us
    ppermute x3, waiting for transfers between devices, group_half(): return lax.ppermute(value, 'grp', [(i, i ^ mask) for i in range(count)])  5.12 us
    pallas_call x1, Pallas kernels, attention(): pl.pallas_call(functools.partial(attention_kernel, band), in_specs=[vmem,...  3.84 us
    pallas_call x1, Pallas kernels, pack(): pl.pallas_call(pack_kernel, grid=(steps,), in_specs=[slot_spec, slot_spec...  3.06 us
  transfers between devices with their start and end apart: 5, of which 4 were waited for; matrix products, arithmetic and copies ran while one was open for 0% of the time, Pallas kernels for 0%

profile of v6, /device:TPU:2, one launch (start us, length us, event | category | flops | bytes accessed | tf_op | source)
XLA Modules:
  0.0 53.2 jit_solution(16918429237992400989)
XLA Ops:
  0.6 0.0 copy-start
  0.6 3.1 %pool_and_pack.1 = bf16[32,136,128]{2,1,0:T(8,128)(2,1)} custom-call(bf16[1,32,4096]{2,1,0:T(8,128)(2,1)} %query_ref.1, bf16[1,32,4096]{2,1,0:T(8,128)(2,1)} %key_ref.1, bf16[1,32,4096]{2,1,0:T(8,128)(2,1)} %value_ref.1, bf16[1,256,4096]{2,1,0:T(8,128)(2,1)} %bytes_ref.1, s32[1,1,32]{2,1,0:T(1,128)} %starts_ref.1), custom_call_target="tpu_custom_call" | custom-call | tf_op jit(solution)/shard_map/pool_and_pack/pallas_call | solution.py:67
  3.7 7.6 %all-to-all-start = ((bf16[32,136,128]{2,1,0:T(8,128)(2,1)}), bf16[32,136,128]{2,1,0:T(8,128)(2,1)S(1)}, u32[]{:S(2)}, u32[]{:S(2)}) async-start(bf16[32,136,128]{2,1,0:T(8,128)(2,1)} %pool_and_pack.1), calls=%async_computation | async-start | bytes 2228224 | tf_op jit(solution)/shard_map/all_to_all | solution.py:270
  11.3 0.0 copy-done
  11.4 15.1 %all-to-all-done.packed_ref = bf16[32,136,128]{2,1,0:T(8,128)(2,1)S(1)} async-done(((bf16[32,136,128]{2,1,0:T(8,128)(2,1)}), bf16[32,136,128]{2,1,0:T(8,128)(2,1)S(1)}, u32[]{:S(2)}, u32[]{:S(2)}) %all-to-all-start) | async-done | bytes 1114144 | tf_op jit(solution)/shard_map/all_to_all | solution.py:270
  26.5 3.8 %attention_grads.1 = (bf16[32,96,128]{2,1,0:T(8,128)(2,1)}, f32[1,128]{1,0:T(1,128)S(1)}) custom-call(bf16[32,136,128]{2,1,0:T(8,128)(2,1)S(1)} %all-to-all-done.packed_ref, f32[1,128]{1,0:T(1,128)S(1)} %constant_dynamic-slice_fusion.gain_ref), custom_call_target="tpu_custom_call" | custom-call | tf_op jit(solution)/shard_map/attention_grads/pallas_call | solution.py:201
  30.3 6.4 %all-to-all-start.1 = ((bf16[32,96,128]{2,1,0:T(8,128)(2,1)}), bf16[32,96,128]{2,1,0:T(8,128)(2,1)S(1)}, u32[]{:S(2)}, u32[]{:S(2)}) async-start(bf16[32,96,128]{2,1,0:T(8,128)(2,1)} %get-tuple-element.10), calls=%async_computation.1 | async-start | bytes 1572864 | tf_op jit(solution)/shard_map/all_to_all | solution.py:273
  36.8 2.0 %collective-permute-start = (f32[1,128]{1,0:T(1,128)S(1)}, f32[1,128]{1,0:T(1,128)S(1)}, u32[]{:S(2)}, u32[]{:S(2)}) collective-permute-start(f32[1,128]{1,0:T(1,128)S(1)} %get-tuple-element.11), channel_id=1, source_target_pairs={{0,32},{32,0},{64,96},{96,64},{128,160},{160,128},{192,224},{224,1... | collective-permute-start | bytes 1544 | tf_op jit(solution)/shard_map/ppermute | solution.py:265
  38.8 1.6 %collective-permute-done = f32[1,128]{1,0:T(1,128)S(1)} collective-permute-done((f32[1,128]{1,0:T(1,128)S(1)}, f32[1,128]{1,0:T(1,128)S(1)}, u32[]{:S(2)}, u32[]{:S(2)}) %collective-permute-start) | collective-permute-done | bytes 544 | tf_op jit(solution)/shard_map/ppermute | solution.py:265
  40.4 5.9 %collective-permute-start.1 = (f32[1,128]{1,0:T(1,128)S(1)}, f32[1,128]{1,0:T(1,128)S(1)}, u32[]{:S(2)}, u32[]{:S(2)}) collective-permute-start(f32[1,128]{1,0:T(1,128)S(1)} %add.10), channel_id=1, source_target_pairs={{0,224},{32,192},{64,160},{96,128},{128,96},{160,64},{192,32},{224... | collective-permute-start | bytes 1544 | tf_op jit(solution)/shard_map/ppermute | solution.py:265
  46.3 1.5 %collective-permute-done.1 = f32[1,128]{1,0:T(1,128)S(1)} collective-permute-done((f32[1,128]{1,0:T(1,128)S(1)}, f32[1,128]{1,0:T(1,128)S(1)}, u32[]{:S(2)}, u32[]{:S(2)}) %collective-permute-start.1) | collective-permute-done | bytes 544 | tf_op jit(solution)/shard_map/ppermute | solution.py:265
  47.8 2.5 %collective-permute-start.2 = (f32[1,128]{1,0:T(1,128)S(1)}, f32[1,128]{1,0:T(1,128)S(1)}, u32[]{:S(2)}, u32[]{:S(2)}) collective-permute-start(f32[1,128]{1,0:T(1,128)S(1)} %add.11.here_ref), channel_id=1, source_target_pairs={{0,64},{32,96},{64,0},{96,32},{128,192},{160,224},{192,128},{224,1... | collective-permute-start | bytes 1544 | tf_op jit(solution)/shard_map/ppermute | solution.py:265
  50.2 2.0 %collective-permute-done.2.other_ref = f32[1,128]{1,0:T(1,128)S(1)} collective-permute-done((f32[1,128]{1,0:T(1,128)S(1)}, f32[1,128]{1,0:T(1,128)S(1)}, u32[]{:S(2)}, u32[]{:S(2)}) %collective-permute-start.2) | collective-permute-done | bytes 544 | tf_op jit(solution)/shard_map/ppermute | solution.py:265
  52.2 0.0 all-to-all-done.1.grads_ref
  52.2 1.0 %unpack_grads.1 = (bf16[1,32,4096]{2,1,0:T(8,128)(2,1)}, bf16[1,32,4096]{2,1,0:T(8,128)(2,1)}, bf16[1,32,4096]{2,1,0:T(8,128)(2,1)}, f32[1,128]{1,0:T(1,128)}) custom-call(bf16[32,96,128]{2,1,0:T(8,128)(2,1)S(1)} %all-to-all-done.1.grads_ref, f32[1,128]{1,0:T(1,128)S(1)} %add.11.here_ref, f32[1,128]{1,0:T(1,128)S(1)} %collective-permute-done.2.other_ref), custom_call_target="tpu_custom_call" | custom-call | tf_op jit(solution)/shard_map/unpack_grads/pallas_call | solution.py:244
  (3 shorter events, 0.0 us)
Async XLA Ops:
  0.6 10.7 %copy-start = (f32[4096]{0:T(1024)S(1)}, f32[4096]{0:T(1024)}, u32[]{:S(2)}) copy-start(f32[4096]{0:T(1024)} %param.11) | copy-start | bytes 49156
  3.7 22.8 %all-to-all-start = ((bf16[32,136,128]{2,1,0:T(8,128)(2,1)}), bf16[32,136,128]{2,1,0:T(8,128)(2,1)S(1)}, u32[]{:S(2)}, u32[]{:S(2)}) async-start(bf16[32,136,128]{2,1,0:T(8,128)(2,1)} %pool_and_pack.1), calls=%async_computation | async-start | bytes 2228224 | tf_op jit(solution)/shard_map/all_to_all | solution.py:270
  30.3 21.9 %all-to-all-start.1 = ((bf16[32,96,128]{2,1,0:T(8,128)(2,1)}), bf16[32,96,128]{2,1,0:T(8,128)(2,1)S(1)}, u32[]{:S(2)}, u32[]{:S(2)}) async-start(bf16[32,96,128]{2,1,0:T(8,128)(2,1)} %get-tuple-element.10), calls=%async_computation.1 | async-start | bytes 1572864 | tf_op jit(solution)/shard_map/all_to_all | solution.py:273
  36.8 3.6 %collective-permute-start = (f32[1,128]{1,0:T(1,128)S(1)}, f32[1,128]{1,0:T(1,128)S(1)}, u32[]{:S(2)}, u32[]{:S(2)}) collective-permute-start(f32[1,128]{1,0:T(1,128)S(1)} %get-tuple-element.11), channel_id=1, source_target_pairs={{0,32},{32,0},{64,96},{96,64},{128,160},{160,128},{192,224},{224,1... | collective-permute-start | bytes 1544 | tf_op jit(solution)/shard_map/ppermute | solution.py:265
  40.4 7.4 %collective-permute-start.1 = (f32[1,128]{1,0:T(1,128)S(1)}, f32[1,128]{1,0:T(1,128)S(1)}, u32[]{:S(2)}, u32[]{:S(2)}) collective-permute-start(f32[1,128]{1,0:T(1,128)S(1)} %add.10), channel_id=1, source_target_pairs={{0,224},{32,192},{64,160},{96,128},{128,96},{160,64},{192,32},{224... | collective-permute-start | bytes 1544 | tf_op jit(solution)/shard_map/ppermute | solution.py:265
  47.8 4.4 %collective-permute-start.2 = (f32[1,128]{1,0:T(1,128)S(1)}, f32[1,128]{1,0:T(1,128)S(1)}, u32[]{:S(2)}, u32[]{:S(2)}) collective-permute-start(f32[1,128]{1,0:T(1,128)S(1)} %add.11.here_ref), channel_id=1, source_target_pairs={{0,64},{32,96},{64,0},{96,32},{128,192},{160,224},{192,128},{224,1... | collective-permute-start | bytes 1544 | tf_op jit(solution)/shard_map/ppermute | solution.py:265
